TPU v7x, 512 devices: a whole 4x4x16 slice. The times are simulated.
512 devices in a mesh: dp: 64 (over y_lo, z, core), tensor: 8 (over x, y_hi).
Axes of the slice: x: 4, y: 4 (y_hi: 2, y_lo: 2; y = y_hi * 2 + y_lo), z: 16, core: 2. Of those that a mesh axis runs over, the one named last changes fastest.
Arguments:
- resp_q: bfloat16 [8192, 8192], P(('dp', 'tensor')), may hold values from -8 to 8
- resp_kv: bfloat16 [8192, 2048], P(('dp', 'tensor')), may hold values from -6 to 6
- prompt_kv: bfloat16 [2048, 2048], P('dp', 'tensor'), may hold values from -6 to 6
- grad_out: bfloat16 [8192, 8192], P(('dp', 'tensor')), may hold values from -6 to 6
- lengths: int32 [128], replicated, may hold values from 8 to 64, as said below
- resp_lists: int32 [64, 2], replicated, may hold values from 0 to 127, as said below
- owner_map: int32 [64], replicated, may hold values from 0 to 63, each once
Outputs:
- attention: bfloat16 [8192, 8192], P(('dp', 'tensor'))
- query_grad: bfloat16 [8192, 8192], P(('dp', 'tensor'))
- response_grad: bfloat16 [8192, 2048], P(('dp', 'tensor'))
- prompt_grad: bfloat16 [2048, 2048], P('dp', 'tensor')
Inputs may be any that keep to these rules, and one draw needn't show every extreme that they name: `lengths`: some response has 8 tokens and some has 64. `resp_lists`: every response appears in exactly one slot.
All inputs are finite; a program needn't handle non-finite values.
Results may differ from a plain program's by a relative error of at most 0.02.
Values may be sent and summed in bfloat16 or wider, within the bound.
A program may use at most 64 MiB of HBM per device.

v0:
```python
import math

import jax
import jax.numpy as jnp
from jax import lax
from jax.sharding import PartitionSpec as P

HQ = 64
KVH = 8
HD = 128
BLOCKS = 8
G = 16


def on_device(resp_q, resp_kv, prompt_kv, grad_out, lengths, resp_lists, owner_map):
    query_rows, grad_rows, own_rows = (
        lax.all_to_all(resp_q, "tensor", split_axis=1, concat_axis=0, tiled=True),
        lax.all_to_all(grad_out, "tensor", split_axis=1, concat_axis=0, tiled=True),
        lax.all_to_all(resp_kv, "tensor", split_axis=1, concat_axis=0, tiled=True),
    )
    slot_count = resp_lists.shape[1]
    block_rows = prompt_kv.shape[0]
    row_width = prompt_kv.shape[1]
    kv_heads = row_width // (2 * HD)
    group_size = HQ // KVH
    slot_rows = query_rows.shape[0] // slot_count
    scale_factor = 1.0 / math.sqrt(HD)
    learner = lax.axis_index("dp")
    chosen = lax.dynamic_index_in_dim(resp_lists, learner, 0, keepdims=False)
    prompt_ids = chosen // G
    positions = jnp.arange(slot_rows)
    live_rows = positions[None, :] < jnp.take(lengths, chosen)[:, None]
    live_mask = live_rows.astype(jnp.bfloat16)
    query = query_rows.reshape(slot_count, slot_rows, kv_heads, group_size, HD)
    cotangent = (
        grad_rows.reshape(slot_count, slot_rows, kv_heads, group_size, HD)
        * live_mask[:, :, None, None, None]
    )
    own_kv = own_rows.reshape(slot_count, slot_rows, kv_heads, 2, HD)
    own_keys = own_kv[:, :, :, 0]
    own_values = own_kv[:, :, :, 1]
    gathered = lax.all_gather(prompt_kv, "dp", axis=0, tiled=True)
    inverse = jnp.argsort(owner_map)
    block_picks = inverse.reshape(-1, BLOCKS)[prompt_ids]
    picked = gathered.reshape(-1, block_rows, row_width)[block_picks]
    prompt_side = picked.reshape(slot_count, BLOCKS * block_rows, kv_heads, 2, HD)
    prompt_keys = prompt_side[:, :, :, 0]
    prompt_values = prompt_side[:, :, :, 1]
    prompt_scores = (
        jnp.einsum("sthgd,skhd->sthgk", query, prompt_keys, preferred_element_type=jnp.float32)
        * scale_factor
    )
    own_scores = (
        jnp.einsum("sthgd,suhd->sthgu", query, own_keys, preferred_element_type=jnp.float32)
        * scale_factor
    )
    allowed = (positions[None, :] <= positions[:, None])[None] & live_rows[:, None, :]
    own_scores = jnp.where(allowed[:, :, None, None, :], own_scores, -jnp.inf)
    row_max = jnp.maximum(prompt_scores.max(-1), own_scores.max(-1))
    prompt_exp = jnp.exp(prompt_scores - row_max[..., None])
    own_exp = jnp.exp(own_scores - row_max[..., None])
    row_total = prompt_exp.sum(-1) + own_exp.sum(-1)
    prompt_probs = prompt_exp / row_total[..., None]
    own_probs = own_exp / row_total[..., None]
    prompt_rounded = prompt_probs.astype(jnp.bfloat16)
    own_rounded = own_probs.astype(jnp.bfloat16)
    mixed = jnp.einsum(
        "sthgk,skhd->sthgd", prompt_rounded, prompt_values, preferred_element_type=jnp.float32
    )
    mixed = mixed + jnp.einsum(
        "sthgu,suhd->sthgd", own_rounded, own_values, preferred_element_type=jnp.float32
    )
    attention = (mixed * live_mask.astype(jnp.float32)[:, :, None, None, None]).astype(jnp.bfloat16)
    attention_rows = attention.reshape(slot_count * slot_rows, kv_heads * group_size * HD)
    attention_out = lax.all_to_all(
        attention_rows, "tensor", split_axis=0, concat_axis=1, tiled=True
    )
    delta = jnp.sum(cotangent.astype(jnp.float32) * attention.astype(jnp.float32), -1)
    prompt_dprob = jnp.einsum(
        "sthgd,skhd->sthgk", cotangent, prompt_values, preferred_element_type=jnp.float32
    )
    own_dprob = jnp.einsum(
        "sthgd,suhd->sthgu", cotangent, own_values, preferred_element_type=jnp.float32
    )
    prompt_ds = (scale_factor * prompt_probs * (prompt_dprob - delta[..., None])).astype(
        jnp.bfloat16
    )
    own_ds = (scale_factor * own_probs * (own_dprob - delta[..., None])).astype(jnp.bfloat16)
    query_grad = jnp.einsum(
        "sthgk,skhd->sthgd", prompt_ds, prompt_keys, preferred_element_type=jnp.float32
    )
    query_grad = (
        query_grad
        + jnp.einsum("sthgu,suhd->sthgd", own_ds, own_keys, preferred_element_type=jnp.float32)
    ).astype(jnp.bfloat16)
    own_dk = jnp.einsum("sthgu,sthgd->suhd", own_ds, query, preferred_element_type=jnp.float32)
    own_dv = jnp.einsum(
        "sthgu,sthgd->suhd", own_rounded, cotangent, preferred_element_type=jnp.float32
    )
    response_grad = jnp.stack([own_dk, own_dv], 3).astype(jnp.bfloat16)
    query_back, response_back = (
        lax.all_to_all(
            query_grad.reshape(slot_count * slot_rows, kv_heads * group_size * HD),
            "tensor",
            split_axis=0,
            concat_axis=1,
            tiled=True,
        ),
        lax.all_to_all(
            response_grad.reshape(slot_count * slot_rows, row_width),
            "tensor",
            split_axis=0,
            concat_axis=1,
            tiled=True,
        ),
    )
    prompt_dk = jnp.einsum(
        "sthgk,sthgd->skhd", prompt_ds, query, preferred_element_type=jnp.float32
    )
    prompt_dv = jnp.einsum(
        "sthgk,sthgd->skhd", prompt_rounded, cotangent, preferred_element_type=jnp.float32
    )
    compact = jnp.stack([prompt_dk, prompt_dv], 3).reshape(
        slot_count, BLOCKS, block_rows, row_width
    )
    owner_table = jnp.zeros((owner_map.shape[0], block_rows, row_width), jnp.float32)
    for slot_index in range(slot_count):
        hit_mask = (owner_map // BLOCKS == prompt_ids[slot_index]).astype(jnp.float32)
        owner_table = (
            owner_table + compact[slot_index][owner_map % BLOCKS] * hit_mask[:, None, None]
        )
    summed = lax.psum_scatter(
        owner_table.reshape(-1, row_width), "dp", scatter_dimension=0, tiled=True
    )
    prompt_grad = summed.astype(jnp.bfloat16)
    return (attention_out, query_back, response_back, prompt_grad)


def solution(mesh):
    return jax.shard_map(
        on_device,
        mesh=mesh,
        in_specs=(
            P(("dp", "tensor"), None),
            P(("dp", "tensor"), None),
            P("dp", "tensor"),
            P(("dp", "tensor"), None),
            P(),
            P(),
            P(),
        ),
        out_specs=(
            P(("dp", "tensor"), None),
            P(("dp", "tensor"), None),
            P(("dp", "tensor"), None),
            P("dp", "tensor"),
        ),
        check_vma=False,
    )
```

profile of v0, /device:TPU:1, one launch (start us, length us, event | category | flops | bytes accessed | tf_op | source)
XLA Modules:
  0.0 379.0 jit_solution(12831816348872523017)
XLA Ops:
  7.9 1.5 copy.141
  9.4 7.5 %all-to-all-start.1 = ((bf16[16,8,256]{2,0,1:T(8,128)(2,1)}), bf16[16,8,256]{2,0,1:T(8,128)(2,1)S(1)}, u32[]{:S(2)}, u32[]{:S(2)}) async-start(bf16[16,8,256]{2,0,1:T(8,128)(2,1)} %bitcast.268), calls=%async_computation.1 | async-start | bytes 131072 | tf_op jit(solution)/shard_map/all_to_all | solution.py:19
  17.1 2.7 sort.17
  20.5 1.3 gather_fusion.2
  22.4 1.7 copy.140
  24.8 1.3 compare_convert_fusion.1
  26.8 6.7 %all-to-all-start = ((bf16[16,8,1024]{2,0,1:T(8,128)(2,1)}), bf16[16,8,1024]{2,0,1:T(8,128)(2,1)S(1)}, u32[]{:S(2)}, u32[]{:S(2)}) async-start(bf16[16,8,1024]{2,0,1:T(8,128)(2,1)} %bitcast.267), calls=%async_computation | async-start | bytes 524288 | tf_op jit(solution)/shard_map/all_to_all | solution.py:17
  35.0 5.7 %all-to-all-done = bf16[16,8,1024]{2,0,1:T(8,128)(2,1)S(1)} async-done(((bf16[16,8,1024]{2,0,1:T(8,128)(2,1)}), bf16[16,8,1024]{2,0,1:T(8,128)(2,1)S(1)}, u32[]{:S(2)}, u32[]{:S(2)}) %all-to-all-start) | async-done | bytes 262176 | tf_op jit(solution)/shard_map/all_to_all | solution.py:17
  40.8 3.4 all-to-all-start.3
  45.2 6.3 %all-to-all-done.3 = bf16[16,8,1024]{2,0,1:T(8,128)(2,1)S(1)} async-done(((bf16[16,8,1024]{2,0,1:T(8,128)(2,1)}), bf16[16,8,1024]{2,0,1:T(8,128)(2,1)S(1)}, u32[]{:S(2)}, u32[]{:S(2)}) %all-to-all-start.3) | async-done | bytes 262176 | tf_op jit(solution)/shard_map/all_to_all | solution.py:18
  52.1 84.4 %all-gather.2.cloned.1.call-done = bf16[2048,256]{1,0:T(8,128)(2,1)} async-done(((bf16[32,256]{1,0:T(8,128)(2,1)}), bf16[2048,256]{1,0:T(8,128)(2,1)}) %all-gather.2.cloned.1.call-update) | async-done | bytes 1048592 | tf_op jit(solution)/shard_map/all_gather | solution.py:42
  136.5 1.8 gather_fusion.1
  141.0 1.0 multiply_reduce_fusion
  144.6 2.0 gather_fusion.3
  146.6 3.0 fusion
  149.6 0.9 copy-done.2
  152.4 6.1 %all-to-all-start.5 = ((bf16[8,16,256]{2,1,0:T(8,128)(2,1)}), bf16[8,16,256]{2,1,0:T(8,128)(2,1)S(1)}, u32[]{:S(2)}, u32[]{:S(2)}) async-start(bf16[8,16,256]{2,1,0:T(8,128)(2,1)} %convert_element_type.88), calls=%async_computation.5 | async-start | bytes 131072 | tf_op jit(solution)/shard_map/all_to_all | solution.py:109
  159.6 5.6 %all-to-all-done.5 = bf16[8,16,256]{2,1,0:T(8,128)(2,1)S(1)} async-done(((bf16[8,16,256]{2,1,0:T(8,128)(2,1)}), bf16[8,16,256]{2,1,0:T(8,128)(2,1)S(1)}, u32[]{:S(2)}, u32[]{:S(2)}) %all-to-all-start.5) | async-done | bytes 65568 | tf_op jit(solution)/shard_map/all_to_all | solution.py:109
  165.2 3.4 all-to-all-start.2
  170.2 5.7 %all-to-all-done.2 = bf16[8,16,1024]{2,1,0:T(8,128)(2,1)S(1)} async-done(((bf16[8,16,1024]{2,1,0:T(8,128)(2,1)}), bf16[8,16,1024]{2,1,0:T(8,128)(2,1)S(1)}, u32[]{:S(2)}, u32[]{:S(2)}) %all-to-all-start.2) | async-done | bytes 262176 | tf_op jit(solution)/shard_map/all_to_all | solution.py:75
  175.9 3.4 all-to-all-start.4
  180.7 5.9 %all-to-all-done.4 = bf16[8,16,1024]{2,1,0:T(8,128)(2,1)S(1)} async-done(((bf16[8,16,1024]{2,1,0:T(8,128)(2,1)}), bf16[8,16,1024]{2,1,0:T(8,128)(2,1)S(1)}, u32[]{:S(2)}, u32[]{:S(2)}) %all-to-all-start.4) | async-done | bytes 262176 | tf_op jit(solution)/shard_map/all_to_all | solution.py:102
  187.3 183.6 %reduce-scatter.2.cloned.1.call-done = f32[32,256]{1,0:T(8,128)} async-done(((f32[2048,256]{1,0:T(8,128)}), f32[32,256]{1,0:T(8,128)}) %reduce-scatter.2.cloned.1.call-update) | async-done | bytes 32784 | tf_op jit(solution)/shard_map/reduce_scatter | solution.py:132
  370.8 1.4 convert_element_type.91
  (101 shorter events, 18.4 us)
Async XLA Ops:
  7.2 9.7 %copy-start = (s32[64,2]{0,1:T(2,128)S(1)}, s32[64,2]{0,1:T(2,128)}, u32[]{:S(2)}) copy-start(s32[64,2]{0,1:T(2,128)} %param.12) | copy-start | bytes 1540
  7.2 27.1 %copy-start.10 = (bf16[16,8192]{1,0:T(8,128)(2,1)S(1)}, bf16[16,8192]{1,0:T(8,128)(2,1)}, u32[]{:S(2)}) copy-start(bf16[16,8192]{1,0:T(8,128)(2,1)} %param.10) | copy-start | bytes 786436
  7.2 129.3 %all-gather.2.cloned.1.call-start = ((), (), s32[]{:S(2)}) async-start(), calls=%async_computation.7 | async-start | bytes 1064960 | tf_op jit(solution)/shard_map/all_gather | solution.py:42
  9.4 17.4 %all-to-all-start.1 = ((bf16[16,8,256]{2,0,1:T(8,128)(2,1)}), bf16[16,8,256]{2,0,1:T(8,128)(2,1)S(1)}, u32[]{:S(2)}, u32[]{:S(2)}) async-start(bf16[16,8,256]{2,0,1:T(8,128)(2,1)} %bitcast.268), calls=%async_computation.1 | async-start | bytes 131072 | tf_op jit(solution)/shard_map/all_to_all | solution.py:19
  26.8 13.9 %all-to-all-start = ((bf16[16,8,1024]{2,0,1:T(8,128)(2,1)}), bf16[16,8,1024]{2,0,1:T(8,128)(2,1)S(1)}, u32[]{:S(2)}, u32[]{:S(2)}) async-start(bf16[16,8,1024]{2,0,1:T(8,128)(2,1)} %bitcast.267), calls=%async_computation | async-start | bytes 524288 | tf_op jit(solution)/shard_map/all_to_all | solution.py:17
  40.8 10.7 %all-to-all-start.3 = ((bf16[16,8,1024]{2,0,1:T(8,128)(2,1)}), bf16[16,8,1024]{2,0,1:T(8,128)(2,1)S(1)}, u32[]{:S(2)}, u32[]{:S(2)}) async-start(bf16[16,8,1024]{2,0,1:T(8,128)(2,1)} %bitcast.266), calls=%async_computation.3 | async-start | bytes 524288 | tf_op jit(solution)/shard_map/all_to_all | solution.py:18
  44.2 326.7 %reduce-scatter.2.cloned.1.call-start = ((), (), s32[]{:S(2)}) async-start(), calls=%async_computation.8 | async-start | bytes 2129920 | tf_op jit(solution)/shard_map/reduce_scatter | solution.py:132
  51.7 90.3 %copy-start.3 = (bf16[2,64,8,128]{3,2,1,0:T(8,128)(2,1)}, bf16[2,64,8,128]{3,2,1,0:T(8,128)(2,1)S(1)}, u32[]{:S(2)}) copy-start(bf16[2,64,8,128]{3,2,1,0:T(8,128)(2,1)S(1)} %bitcast_multiply_fusion.2) | copy-start | bytes 786436
  138.7 0.9 copy-start.6
  139.7 2.3 copy-start.11
  139.8 2.2 copy-start.1
  142.6 1.1 copy-start.8
  144.6 2.0 copy-start.13
  144.6 2.0 copy-start.14
  149.6 0.9 copy-start.2
  149.6 1.2 copy-start.4
  149.6 1.4 copy-start.12
  149.6 1.4 copy-start.16
  150.8 7.8 %copy-start.5 = (bf16[2,64,1,8,128]{4,1,3,0,2:T(8,128)(2,1)S(1)}, bf16[2,64,1,8,128]{4,1,3,0,2:T(8,128)(2,1)}, u32[]{:S(2)}) copy-start(bf16[2,64,1,8,128]{4,1,3,0,2:T(8,128)(2,1)} %get-tuple-element.28) | copy-start | bytes 786436
  151.0 17.6 %copy-start.7 = (bf16[2,256,1,1,128]{4,3,1,0,2:T(2,128)(2,1)S(1)}, bf16[2,256,1,1,128]{4,3,1,0,2:T(2,128)(2,1)}, u32[]{:S(2)}) copy-start(bf16[2,256,1,1,128]{4,3,1,0,2:T(2,128)(2,1)} %copy-done.6) | copy-start | bytes 393220
  151.0 17.6 %copy-start.9 = (bf16[2,64,8,256]{3,1,2,0:T(8,128)(2,1)S(1)}, bf16[2,64,8,256]{3,1,2,0:T(8,128)(2,1)}, u32[]{:S(2)}) copy-start(bf16[2,64,8,256]{3,1,2,0:T(8,128)(2,1)} %copy-done.8) | copy-start | bytes 1572868
  152.4 12.7 %all-to-all-start.5 = ((bf16[8,16,256]{2,1,0:T(8,128)(2,1)}), bf16[8,16,256]{2,1,0:T(8,128)(2,1)S(1)}, u32[]{:S(2)}, u32[]{:S(2)}) async-start(bf16[8,16,256]{2,1,0:T(8,128)(2,1)} %convert_element_type.88), calls=%async_computation.5 | async-start | bytes 131072 | tf_op jit(solution)/shard_map/all_to_all | solution.py:109
  165.2 10.7 %all-to-all-start.2 = ((bf16[8,16,1024]{2,1,0:T(8,128)(2,1)}), bf16[8,16,1024]{2,1,0:T(8,128)(2,1)S(1)}, u32[]{:S(2)}, u32[]{:S(2)}) async-start(bf16[8,16,1024]{2,1,0:T(8,128)(2,1)} %all_to_all.82), calls=%async_computation.2 | async-start | bytes 524288 | tf_op jit(solution)/shard_map/all_to_all | solution.py:75
  175.9 10.6 %all-to-all-start.4 = ((bf16[8,16,1024]{2,1,0:T(8,128)(2,1)}), bf16[8,16,1024]{2,1,0:T(8,128)(2,1)S(1)}, u32[]{:S(2)}, u32[]{:S(2)}) async-start(bf16[8,16,1024]{2,1,0:T(8,128)(2,1)} %all_to_all.89), calls=%async_computation.4 | async-start | bytes 524288 | tf_op jit(solution)/shard_map/all_to_all | solution.py:102
  (1 other events, 0.6 us)
Sparse Core Ops, SparseCore 0:
  10.2 126.2 all-gather.1
  149.8 221.0 reduce-scatter.1
where the time goes:
time: 383 us; the launch traced here: 379 us
  waiting for transfers between devices  298 us (78%)
  starting transfers between devices  30.6 us (8%)
  local copies, waits for them, and re-layouts  20.2 us (5%)
  between operations  14.5 us (4%)
  other arithmetic  11.1 us (3%)
  matrix products  4.86 us (1%)
    reduce_scatter x1, waiting for transfers between devices, on_device(): lax.psum_scatter(owner_table.reshape(-1, row_width), 'dp', scatter_dimens...  184 us
    all_gather x1, waiting for transfers between devices, on_device(): gathered = lax.all_gather(prompt_kv, 'dp', axis=0, tiled=True)  84.4 us
  transfers between devices with their start and end apart: 8, of which 7 were waited for; matrix products, arithmetic and copies ran while one was open for 5% of the time, Pallas kernels for 0%

commit v1 on v0

v1 whole, which is shorter than its diff:
```python
import math

import jax
import jax.numpy as jnp
from jax import lax
from jax.experimental import pallas as pl
from jax.experimental.pallas import tpu as pltpu
from jax.sharding import PartitionSpec as P

MESH = pl.DeviceIdType.MESH
BF = jnp.bfloat16
F32 = jnp.float32
HD = 128
BLOCKS = 8
G = 16
Z = 16
T = 8
SLOTS = 2
LR = 64
GROUP = 8
BR = 32
PL = BLOCKS * BR
KEYS = PL + LR
HW = GROUP * HD
KW = 2 * HD
SCALE = 1.0 / math.sqrt(HD)
NEAR = (4, -4, 3, -3, 2, -2, 1, -1)


def dot(a, b, dims):
    return lax.dot_general(a, b, (dims, ((), ())), preferred_element_type=F32)


def kernel(
    q_in, kv_in, pkv_in, g_in, lengths, lists, owners,
    att_out, qg_out, rg_out, pg_out,
    qbuf, gbuf, kvbuf, obuf, dqbuf, rgbuf,
    table, kcat, vcat, probs_t, dscore_t,
    compact, part, direct, relay_a, relay_b, relayed, rsum, ysum,
    loc_sem, a2a_s, a2a_r, agz_s, agz_r, agy_s, agy_r, agc_s, agc_r,
    back_s, back_r, cc_s, cc_r, rs_s, rs_r, fy_s, fy_r,
):
    dp = lax.axis_index("dp")
    t = lax.axis_index("tensor")
    core = lax.rem(dp, 2)
    z = lax.rem(dp // 2, Z)
    y = dp // (2 * Z)

    def at_z(d):
        return (y * (2 * Z) + lax.rem(z + d + Z, Z) * 2 + core, t)

    other_core = (y * (2 * Z) + z * 2 + (1 - core), t)
    other_y = ((1 - y) * (2 * Z) + z * 2 + core, t)
    peers = [(lax.rem(t + k, T)) for k in range(1, T)]

    def remote(src, dst, s, r, device):
        return pltpu.make_async_remote_copy(
            src_ref=src, dst_ref=dst, send_sem=s, recv_sem=r, device_id=device, device_id_type=MESH
        )

    def columns(width, index):
        return pl.ds(pl.multiple_of(index * width, width), width)

    local = [
        pltpu.make_async_copy(pkv_in, table.at[0, 0, 8], loc_sem.at[0]),
        pltpu.make_async_copy(q_in.at[:, columns(HW, t)], qbuf.at[t], loc_sem.at[1]),
        pltpu.make_async_copy(g_in.at[:, columns(HW, t)], gbuf.at[t], loc_sem.at[2]),
        pltpu.make_async_copy(kv_in.at[:, columns(KW, t)], kvbuf.at[t], loc_sem.at[3]),
    ]
    for copy in local:
        copy.start()
    barrier = pltpu.get_barrier_semaphore()
    greeted = [at_z(d) for d in NEAR] + [other_core, other_y] + [(dp, p) for p in peers]
    for device in greeted:
        pl.semaphore_signal(barrier, inc=1, device_id=device, device_id_type=MESH)
    pl.semaphore_wait(barrier, len(greeted))

    def gather(slot, d):
        dst_slot = slot - d
        src = pkv_in if slot == 8 else table.at[0, 0, slot]
        return remote(src, table.at[0, 0, dst_slot], agz_s.at[dst_slot], agz_r.at[dst_slot], at_z(d))

    sends = []
    step1 = {d: gather(8, d) for d in NEAR}
    for d in NEAR:
        step1[d].start()
        sends.append(step1[d])

    a2a = []
    for i, p in enumerate(peers):
        for a, (src, dst, width) in enumerate(((kv_in, kvbuf, KW), (q_in, qbuf, HW), (g_in, gbuf, HW))):
            copy = remote(src.at[:, columns(width, p)], dst.at[t], a2a_s.at[a, i], a2a_r.at[a, i], (dp, p))
            copy.start()
            a2a.append(copy)

    resp = [lists[dp, s] for s in range(SLOTS)]
    prompt = [lax.div(a, G) for a in resp]
    length = [lengths[a] for a in resp]

    def find(j, found):
        code = owners[j]
        return tuple(
            jnp.where(code == prompt[s] * BLOCKS + b, j, found[s * BLOCKS + b])
            for s in range(SLOTS)
            for b in range(BLOCKS)
        )

    found = lax.fori_loop(0, 4 * Z, find, tuple(jnp.int32(0) for _ in range(SLOTS * BLOCKS)))

    step1[4].wait_recv()
    for d in (4, 3, 2, 1):
        copy = gather(4, d)
        copy.start()
        sends.append(copy)
    step1[-4].wait_recv()
    for d in (-3, -2, -1):
        copy = gather(12, d)
        copy.start()
        sends.append(copy)
    local[0].wait()
    ranges = (pl.ds(4, 9), pl.ds(0, 4), pl.ds(13, 3))
    over_y = [
        remote(table.at[0, 0, r], table.at[1, 0, r], agy_s.at[i], agy_r.at[i], other_y)
        for i, r in enumerate(ranges)
    ]
    over_core = [
        [
            remote(table.at[a, 0, r], table.at[a, 1, r], agc_s.at[a, i], agc_r.at[a, i], other_core)
            for i, r in enumerate(ranges)
        ]
        for a in range(2)
    ]
    for d in NEAR[2:]:
        step1[d].wait_recv()
    over_y[0].start()
    over_core[0][0].start()
    for i, slots in ((1, (3, 2, 1, 0)), (2, (13, 14, 15))):
        for slot in slots:
            gather(slot, 0).wait_recv()
        over_y[i].start()
        over_core[0][i].start()
    for i in range(3):
        over_y[i].wait_recv()
        over_core[1][i].start()
    for copy in local[1:]:
        copy.wait()
    for copy in a2a:
        copy.wait_recv()
    for i in range(3):
        over_core[0][i].wait_recv()
    for i in range(3):
        over_core[1][i].wait_recv()

    def stacked(buf, s, first, heads):
        cols = [buf[4 * s : 4 * s + 4, :, pl.ds(pl.multiple_of(first + h * HD, HD), HD)].reshape(LR, HD) for h in range(heads)]
        return jnp.concatenate(cols, axis=0)

    half = GROUP // 2
    wide = half * LR
    for s in range(SLOTS):
        n = length[s]
        row = lax.broadcasted_iota(jnp.int32, (LR, HW), 0)
        masked = jnp.where(row < n, gbuf[4 * s : 4 * s + 4].reshape(LR, HW).astype(F32), 0.0)
        gbuf[4 * s : 4 * s + 4] = masked.astype(BF).reshape(4, 16, HW)
        for b in range(BLOCKS):
            j = found[s * BLOCKS + b]
            jy, jz, jc = lax.div(j, 2 * Z), lax.rem(lax.div(j, 2), Z), lax.rem(j, 2)
            block = table[jnp.where(jy == y, 0, 1), jnp.where(jc == core, 0, 1), lax.rem(jz - z + 8 + Z, Z)]
            kcat[b * BR : (b + 1) * BR] = block[:, :HD]
            vcat[b * BR : (b + 1) * BR] = block[:, HD:]
        own = kvbuf[4 * s : 4 * s + 4].reshape(LR, KW)
        kcat[PL:] = own[:, :HD]
        vcat[PL:] = own[:, HD:]
        keys, values = kcat[...], vcat[...]

        def part_of(h, _, s=s, n=n, keys=keys, values=values):
            q = stacked(qbuf, s, h * half * HD, half)
            g = stacked(gbuf, s, h * half * HD, half)
            scores = dot(keys, q, ((1,), (1,))) * SCALE
            u = lax.broadcasted_iota(jnp.int32, (LR, wide), 0)
            at = lax.rem(lax.broadcasted_iota(jnp.int32, (LR, wide), 1), LR)
            own_scores = jnp.where((u <= at) & (u < n), scores[PL:], -jnp.inf)
            scores = jnp.concatenate([scores[:PL], own_scores], axis=0)
            top = jnp.max(scores, axis=0, keepdims=True)
            e = jnp.exp(scores - top)
            probs = e * (1.0 / jnp.sum(e, axis=0, keepdims=True))
            rounded = probs.astype(BF)
            dprob = dot(values, g, ((1,), (1,)))
            delta = jnp.sum(rounded.astype(F32) * dprob, axis=0, keepdims=True)
            dscore = (probs * (dprob - delta) * SCALE).astype(BF)
            at_cols = pl.ds(pl.multiple_of(h * wide, wide), wide)
            probs_t[:, at_cols] = rounded
            dscore_t[:, at_cols] = dscore
            out = dot(rounded, values, ((0,), (0,)))
            dq = dot(dscore, keys, ((0,), (0,)))
            live = lax.broadcasted_iota(jnp.int32, (LR, HD), 0) < n
            for i in range(half):
                head = pl.ds(pl.multiple_of(h * half * HD + i * HD, HD), HD)
                rows = slice(i * LR, (i + 1) * LR)
                obuf[4 * s : 4 * s + 4, :, head] = jnp.where(live, out[rows], 0.0).astype(BF).reshape(4, 16, HD)
                dqbuf[4 * s : 4 * s + 4, :, head] = dq[rows].astype(BF).reshape(4, 16, HD)
            return 0

        lax.fori_loop(0, 2, part_of, 0)
        dk = dot(dscore_t[...], stacked(qbuf, s, 0, GROUP), ((1,), (0,)))
        dv = dot(probs_t[...], stacked(gbuf, s, 0, GROUP), ((1,), (0,)))
        both = jnp.concatenate([dk, dv], axis=1).astype(BF)
        for b in range(BLOCKS):
            compact[0, s, b] = both[b * BR : (b + 1) * BR]
        rgbuf[4 * s : 4 * s + 4] = both[PL:].reshape(4, 16, KW)
        copy = remote(compact.at[0, s], compact.at[1, s], cc_s.at[s], cc_r.at[s], other_core)
        copy.start()
        sends.append(copy)

    back = []
    for i, p in enumerate(peers):
        for a, (src, dst_ref, width) in enumerate(((obuf, att_out, HW), (dqbuf, qg_out, HW), (rgbuf, rg_out, KW))):
            copy = remote(src.at[p], dst_ref.at[:, columns(width, t)], back_s.at[a, i], back_r.at[a, i], (dp, p))
            copy.start()
            back.append(copy)
    stay = [
        pltpu.make_async_copy(src.at[t], dst_ref.at[:, columns(width, t)], loc_sem.at[4 + a])
        for a, (src, dst_ref, width) in enumerate(((obuf, att_out, HW), (dqbuf, qg_out, HW), (rgbuf, rg_out, KW)))
    ]
    for copy in stay:
        copy.start()

    for s in range(SLOTS):
        remote(compact.at[0, s], compact.at[1, s], cc_s.at[s], cc_r.at[s], other_core).wait_recv()
    learner2 = dp + 1 - 2 * core
    slot_prompts = prompt + [lax.div(lists[learner2, s], G) for s in range(SLOTS)]

    def fill(k, _):
        for yy in range(2):
            code = owners[yy * (2 * Z) + lax.rem(z + k + 8, Z) * 2 + core]
            p, b = lax.div(code, BLOCKS), lax.rem(code, BLOCKS)
            total = jnp.zeros((BR, KW), F32)
            for c in range(2):
                for s in range(SLOTS):
                    hit = slot_prompts[c * SLOTS + s] == p
                    total = total + jnp.where(hit, compact[c, s, b].astype(F32), 0.0)
            part[k, yy] = total.astype(BF)
        return 0

    lax.fori_loop(0, Z, fill, 0)

    rs = []

    def rs_send(i, src, dst_ref, d):
        copy = remote(src, dst_ref, rs_s.at[i], rs_r.at[i], at_z(d))
        copy.start()
        rs.append(copy)
        sends.append(copy)

    for i, d in enumerate((4, 3, 2, 1)):
        rs_send(i, part.at[(8 + d + 4) % Z], relay_a.at[i], d)
    for i, d in enumerate((-3, -2, -1)):
        rs_send(4 + i, part.at[8 + d - 4], relay_b.at[i], d)
    for i, d in enumerate((3, -3, 2, -2, 1, -1)):
        rs_send(7 + i, part.at[8 + d], direct.at[i], d)
    for copy in rs[:4]:
        copy.wait_recv()
    total = part[12].astype(F32)
    for i in range(4):
        total = total + relay_a[i].astype(F32)
    part[12] = total.astype(BF)
    rs_send(13, part.at[12], relayed.at[0], 4)
    for copy in rs[4:7]:
        copy.wait_recv()
    total = part[4].astype(F32)
    for i in range(3):
        total = total + relay_b[i].astype(F32)
    part[4] = total.astype(BF)
    rs_send(14, part.at[4], relayed.at[1], -4)
    for copy in rs[7:13]:
        copy.wait_recv()
    total = part[8].astype(F32)
    for i in range(6):
        total = total + direct[i].astype(F32)
    for i in range(2):
        rs[13 + i].wait_recv()
        total = total + relayed[i].astype(F32)
    rsum[...] = total
    copy = remote(rsum.at[1 - y], ysum, fy_s.at[0], fy_r.at[0], other_y)
    copy.start()
    sends.append(copy)
    copy.wait_recv()
    pg_out[...] = (rsum[y] + ysum[...]).astype(BF)

    for copy in back:
        copy.wait_recv()
    for copy in stay:
        copy.wait()
    for copy in sends + a2a + back + over_y + over_core[0] + over_core[1]:
        copy.wait_send()


def on_device(resp_q, resp_kv, prompt_kv, grad_out, lengths, resp_lists, owner_map):
    anywhere = pl.BlockSpec(memory_space=pl.ANY)
    scalars = pl.BlockSpec(memory_space=pltpu.SMEM)
    rows = resp_q.shape[0]
    dma = pltpu.SemaphoreType.DMA
    return pl.pallas_call(
        kernel,
        name="attention",
        out_shape=(
            jax.ShapeDtypeStruct(resp_q.shape, BF),
            jax.ShapeDtypeStruct(resp_q.shape, BF),
            jax.ShapeDtypeStruct(resp_kv.shape, BF),
            jax.ShapeDtypeStruct(prompt_kv.shape, BF),
        ),
        in_specs=[anywhere, anywhere, anywhere, anywhere, scalars, scalars, scalars],
        out_specs=(anywhere, anywhere, anywhere, pl.BlockSpec(memory_space=pltpu.VMEM)),
        scratch_shapes=[
            pltpu.VMEM((T, rows, HW), BF),
            pltpu.VMEM((T, rows, HW), BF),
            pltpu.VMEM((T, rows, KW), BF),
            pltpu.VMEM((T, rows, HW), BF),
            pltpu.VMEM((T, rows, HW), BF),
            pltpu.VMEM((T, rows, KW), BF),
            pltpu.VMEM((2, 2, Z, BR, KW), BF),
            pltpu.VMEM((KEYS, HD), BF),
            pltpu.VMEM((KEYS, HD), BF),
            pltpu.VMEM((KEYS, GROUP * LR), BF),
            pltpu.VMEM((KEYS, GROUP * LR), BF),
            pltpu.VMEM((2, SLOTS, BLOCKS, BR, KW), BF),
            pltpu.VMEM((Z, 2, BR, KW), BF),
            pltpu.VMEM((6, 2, BR, KW), BF),
            pltpu.VMEM((4, 2, BR, KW), BF),
            pltpu.VMEM((3, 2, BR, KW), BF),
            pltpu.VMEM((2, 2, BR, KW), BF),
            pltpu.VMEM((2, BR, KW), F32),
            pltpu.VMEM((BR, KW), F32),
            dma((7,)),
            dma((3, T - 1)),
            dma((3, T - 1)),
            dma((Z,)),
            dma((Z,)),
            dma((3,)),
            dma((3,)),
            dma((2, 3)),
            dma((2, 3)),
            dma((3, T - 1)),
            dma((3, T - 1)),
            dma((SLOTS,)),
            dma((SLOTS,)),
            dma((15,)),
            dma((15,)),
            dma((1,)),
            dma((1,)),
        ],
        compiler_params=pltpu.CompilerParams(
            collective_id=0, has_side_effects=True, vmem_limit_bytes=40 * 1024 * 1024
        ),
    )(resp_q, resp_kv, prompt_kv, grad_out, lengths, resp_lists, owner_map)


def solution(mesh):
    rows = P(("dp", "tensor"), None)
    return jax.shard_map(
        on_device,
        mesh=mesh,
        in_specs=(rows, rows, P("dp", "tensor"), rows, P(), P(), P()),
        out_specs=(rows, rows, rows, P("dp", "tensor")),
        check_vma=False,
    )
```

time: 383 us -> 64.5 us (0.17)
  the two profiles are of different devices: /device:TPU:1 before, /device:TPU:8 now
where the time goes in v1:
time: 64.5 us; the launch traced here: 64.2 us
  Pallas kernels  57.4 us (89%)
  local copies, waits for them, and re-layouts  6.17 us (10%)
  between operations  0.69 us (1%)
    pallas_call x1, Pallas kernels, on_device(): pl.pallas_call(kernel, name='attention', out_shape=(jax.ShapeDtypeStruct(...  57.4 us
    unnamed x17, local copies, waits for them, and re-layouts  6.17 us

profile of v1, /device:TPU:8, one launch (start us, length us, event | category | flops | bytes accessed | tf_op | source)
XLA Modules:
  0.0 64.2 jit_solution(14962387192704041107)
XLA Ops:
  0.6 0.0 copy-start.5
  0.6 0.0 copy-start.4
  0.7 0.0 copy-start.3
  0.7 0.8 %copy.11.lists = s32[64,2]{1,0:T(8,128)S(1)} copy(s32[64,2]{0,1:T(2,128)} %param.12) | data formatting | bytes 1024 | tf_op args[5]
  1.4 0.0 copy-done.5
  1.5 0.0 copy-done.4
  1.5 0.0 copy-done.3
  1.5 0.0 copy-start
  1.5 0.9 %copy-done = bf16[16,8192]{1,0:T(8,128)(2,1)S(1)} copy-done((bf16[16,8192]{1,0:T(8,128)(2,1)S(1)}, bf16[16,8192]{1,0:T(8,128)(2,1)}, u32[]{:S(2)}) %copy-start) | copy-done | bytes 262168
  2.4 0.0 copy-start.1
  2.4 0.9 %copy-done.1 = bf16[16,8192]{1,0:T(8,128)(2,1)S(1)} copy-done((bf16[16,8192]{1,0:T(8,128)(2,1)S(1)}, bf16[16,8192]{1,0:T(8,128)(2,1)}, u32[]{:S(2)}) %copy-start.1) | copy-done | bytes 262168
  3.4 0.0 copy-start.2
  3.4 0.8 %copy-done.2 = bf16[16,2048]{1,0:T(8,128)(2,1)S(1)} copy-done((bf16[16,2048]{1,0:T(8,128)(2,1)S(1)}, bf16[16,2048]{1,0:T(8,128)(2,1)}, u32[]{:S(2)}) %copy-start.2) | copy-done | bytes 65560
  4.2 57.4 %attention.1 = (bf16[16,8192]{1,0:T(8,128)(2,1)S(1)}, bf16[16,8192]{1,0:T(8,128)(2,1)S(1)}, bf16[16,2048]{1,0:T(8,128)(2,1)S(1)}, bf16[32,256]{1,0:T(8,128)(2,1)S(1)}) custom-call(bf16[16,8192]{1,0:T(8,128)(2,1)S(1)} %copy-done, bf16[16,2048]{1,0:T(8,128)(2,1)S(1)} %copy-done.2, bf16[32,256]{1,0:T(8,128)(2,1)S(1)} %copy-done.3, ...), custom_call_target="tpu_custom_call" | custom-call | tf_op jit(solution)/shard_map/attention/pallas_call | solution.py:303
  61.6 0.7 %copy.16 = bf16[16,8192]{1,0:T(8,128)(2,1)} copy(bf16[16,8192]{1,0:T(8,128)(2,1)S(1)} %get-tuple-element.8) | data formatting | bytes 524288
  62.3 0.7 %copy.17 = bf16[16,8192]{1,0:T(8,128)(2,1)} copy(bf16[16,8192]{1,0:T(8,128)(2,1)S(1)} %get-tuple-element.9) | data formatting | bytes 524288
  63.0 0.6 copy.18
  63.6 0.6 copy.19
Async XLA Ops:
  0.6 0.8 %copy-start.5 = (s32[64]{0:T(128)S(1)}, s32[64]{0:T(128)}, u32[]{:S(2)}) copy-start(s32[64]{0:T(128)} %owners.1) | copy-start | bytes 772
  0.6 0.8 %copy-start.4 = (s32[128]{0:T(128)S(1)}, s32[128]{0:T(128)}, u32[]{:S(2)}) copy-start(s32[128]{0:T(128)} %lengths.1) | copy-start | bytes 1540
  0.7 0.8 %copy-start.3 = (bf16[32,256]{1,0:T(8,128)(2,1)S(1)}, bf16[32,256]{1,0:T(8,128)(2,1)}, u32[]{:S(2)}) copy-start(bf16[32,256]{1,0:T(8,128)(2,1)} %pkv_in.1) | copy-start | bytes 49156
  1.5 1.0 %copy-start = (bf16[16,8192]{1,0:T(8,128)(2,1)S(1)}, bf16[16,8192]{1,0:T(8,128)(2,1)}, u32[]{:S(2)}) copy-start(bf16[16,8192]{1,0:T(8,128)(2,1)} %q_in.1) | copy-start | bytes 786436
  2.4 0.9 %copy-start.1 = (bf16[16,8192]{1,0:T(8,128)(2,1)S(1)}, bf16[16,8192]{1,0:T(8,128)(2,1)}, u32[]{:S(2)}) copy-start(bf16[16,8192]{1,0:T(8,128)(2,1)} %g_in.1) | copy-start | bytes 786436
  3.4 0.8 %copy-start.2 = (bf16[16,2048]{1,0:T(8,128)(2,1)S(1)}, bf16[16,2048]{1,0:T(8,128)(2,1)}, u32[]{:S(2)}) copy-start(bf16[16,2048]{1,0:T(8,128)(2,1)} %kv_in.1) | copy-start | bytes 196612

commit v2 on v1

v2 whole, which is shorter than its diff:
```python
import math

import jax
import jax.numpy as jnp
from jax import lax
from jax.experimental import pallas as pl
from jax.experimental.pallas import tpu as pltpu
from jax.sharding import PartitionSpec as P

MESH = pl.DeviceIdType.MESH
BF = jnp.bfloat16
F32 = jnp.float32
HD = 128
BLOCKS = 8
G = 16
Z = 16
T = 8
SLOTS = 2
LR = 64
GROUP = 8
BR = 32
PL = BLOCKS * BR
KEYS = PL + LR
HW = GROUP * HD
KW = 2 * HD
HALF = GROUP // 2
WIDE = HALF * LR
SCALE = 1.0 / math.sqrt(HD)
NEAR = (4, -4, 3, -3, 2, -2, 1, -1)
K, V = 0, 1


def dot(a, b, dims):
    return lax.dot_general(a, b, (dims, ((), ())), preferred_element_type=F32)


def kernel(
    q_in, kv_in, pkv_in, g_in, lengths_in, lists_in, owners_in,
    att_out, qg_out, rg_out, pg_out,
    qbuf, gbuf, kvbuf, obuf, dqbuf, rgbuf,
    table_k, table_v, kcat, vcat, probs_f, probs_t, dscore_t,
    compact_k, compact_v, part, direct, relay_a, relay_b, relayed, rsum, ysum, lengths, lists, owners,
    loc, a2a_s, a2a_r, agz_s, agz_r, agy_s, agy_r, agc_s, agc_r, back_s, back_r, cc_s, cc_r, rs_s, rs_r, fy_s, fy_r,
):
    table, compact = (table_k, table_v), (compact_k, compact_v)
    dp = lax.axis_index("dp")
    t = lax.axis_index("tensor")
    core = lax.rem(dp, 2)
    z = lax.rem(dp // 2, Z)
    y = dp // (2 * Z)

    def at_z(d):
        return (y * (2 * Z) + lax.rem(z + d + Z, Z) * 2 + core, t)

    other_core = (y * (2 * Z) + z * 2 + (1 - core), t)
    other_y = ((1 - y) * (2 * Z) + z * 2 + core, t)
    peers = [lax.rem(t + k, T) for k in range(1, T)]

    def send(src, dst, s, r, device):
        pltpu.make_async_remote_copy(
            src_ref=src, dst_ref=dst, send_sem=s, recv_sem=r, device_id=device, device_id_type=MESH
        ).start()

    def wait(ref, sem):
        pltpu.make_async_copy(ref, ref, sem).wait()

    def columns(width, index):
        return pl.ds(pl.multiple_of(index * width, width), width)

    barrier = pltpu.get_barrier_semaphore()
    greeted = [(dp, p) for p in peers] + [at_z(d) for d in NEAR] + [other_y, other_core]
    for device in greeted:
        pl.semaphore_signal(barrier, inc=1, device_id=device, device_id_type=MESH)
    local = [
        pltpu.make_async_copy(pkv_in.at[:, :HD], table[K].at[0, 0, 8], loc.at[0]),
        pltpu.make_async_copy(pkv_in.at[:, HD:], table[V].at[0, 0, 8], loc.at[1]),
        pltpu.make_async_copy(kv_in.at[:, columns(KW, t)], kvbuf.at[t], loc.at[2]),
        pltpu.make_async_copy(q_in.at[:, columns(HW, t)], qbuf.at[t], loc.at[3]),
        pltpu.make_async_copy(g_in.at[:, columns(HW, t)], gbuf.at[t], loc.at[4]),
        pltpu.make_async_copy(lengths_in, lengths, loc.at[5]),
        pltpu.make_async_copy(lists_in, lists, loc.at[6]),
        pltpu.make_async_copy(owners_in, owners, loc.at[7]),
    ]
    for copy in local:
        copy.start()
    for copy in local[:2]:
        copy.wait()
    pl.semaphore_wait(barrier, len(greeted))

    def arrival(slot):
        return 0 if slot == 4 else 1 if slot == 12 else 2 if 4 < slot < 12 else 3 if slot < 4 else 4

    def gather(kv, slot, d):
        to = slot - d
        send(table[kv].at[0, 0, slot], table[kv].at[0, 0, to], agz_s.at[kv], agz_r.at[kv, arrival(to)], at_z(d))

    def to_heads(a, src, dst, width):
        for p in peers:
            send(src.at[:, columns(width, p)], dst.at[t], a2a_s.at[a], a2a_r.at[a], (dp, p))

    for d in NEAR:
        gather(K, 8, d)
    to_heads(0, kv_in, kvbuf, KW)
    for d in NEAR:
        gather(V, 8, d)
    to_heads(1, q_in, qbuf, HW)
    to_heads(2, g_in, gbuf, HW)

    for kv in (K, V):
        wait(table[kv].at[0, 0, 4], agz_r.at[kv, 0])
        for d in (4, 3, 2, 1):
            gather(kv, 4, d)
        wait(table[kv].at[0, 0, 12], agz_r.at[kv, 1])
        for d in (-3, -2, -1):
            gather(kv, 12, d)

    groups = (pl.ds(4, 9), pl.ds(0, 4), pl.ds(13, 3))

    def over_y(kv, i):
        r = groups[i]
        send(table[kv].at[0, 0, r], table[kv].at[1, 0, r], agy_s.at[kv], agy_r.at[kv, i], other_y)

    def over_core(kv, a, i):
        r = groups[i]
        send(table[kv].at[a, 0, r], table[kv].at[a, 1, r], agc_s.at[kv], agc_r.at[kv], other_core)

    for kv in (K, V):
        wait(table[kv].at[0, 0, pl.ds(4, 6)], agz_r.at[kv, 2])
        over_y(kv, 0)
        over_core(kv, 0, 0)

    for copy in local[5:]:
        copy.wait()
    resp = [lists[s, dp] for s in range(SLOTS)]
    prompt = [lax.div(a, G) for a in resp]
    length = [lengths[a] for a in resp]

    def find(j, found):
        code = owners[j]
        return tuple(
            jnp.where(code == prompt[s] * BLOCKS + b, j, found[s * BLOCKS + b])
            for s in range(SLOTS)
            for b in range(BLOCKS)
        )

    found = lax.fori_loop(0, 4 * Z, find, tuple(jnp.int32(0) for _ in range(SLOTS * BLOCKS)), unroll=4)

    def pick(cat, kv, s):
        for b in range(BLOCKS):
            j = found[s * BLOCKS + b]
            jy, jz, jc = lax.div(j, 2 * Z), lax.rem(lax.div(j, 2), Z), lax.rem(j, 2)
            block = table[kv][jnp.where(jy == y, 0, 1), jnp.where(jc == core, 0, 1), lax.rem(jz - z + 8 + Z, Z)]
            cat[s, b * BR : (b + 1) * BR] = block

    for kv in (K, V):
        for i in (1, 2):
            wait(table[kv].at[0, 0, groups[i]], agz_r.at[kv, 2 + i])
            over_y(kv, i)
            over_core(kv, 0, i)
    for kv in (K, V):
        for i in range(3):
            wait(table[kv].at[1, 0, groups[i]], agy_r.at[kv, i])
            over_core(kv, 1, i)
    for copy in local[2:5]:
        copy.wait()
    for a, buf in enumerate((kvbuf, qbuf, gbuf)):
        wait(buf.at[pl.ds(0, T - 1)], a2a_r.at[a])
    for s in range(SLOTS):
        row = lax.broadcasted_iota(jnp.int32, (LR, HW), 0)
        masked = jnp.where(row < length[s], gbuf[4 * s : 4 * s + 4].reshape(LR, HW).astype(F32), 0.0)
        gbuf[4 * s : 4 * s + 4] = masked.astype(BF).reshape(4, 16, HW)
        own = kvbuf[4 * s : 4 * s + 4].reshape(LR, KW)
        kcat[s, PL:] = own[:, :HD]
        vcat[s, PL:] = own[:, HD:]

    def stacked(buf, s, first, heads):
        cols = [buf[4 * s : 4 * s + 4, :, pl.ds(pl.multiple_of(first + h * HD, HD), HD)].reshape(LR, HD) for h in range(heads)]
        return jnp.concatenate(cols, axis=0)

    def hand_over(kv, s, grad):
        out = grad.astype(BF)
        compact[kv][0, s] = out[:PL].reshape(BLOCKS, BR, HD)
        rgbuf[4 * s : 4 * s + 4, :, kv * HD : (kv + 1) * HD] = out[PL:].reshape(4, 16, HD)
        send(compact[kv].at[0, s], compact[kv].at[1, s], cc_s.at[kv], cc_r.at[kv], other_core)

    wait(table[K].at[:, 1], agc_r.at[K])
    for s in range(SLOTS):
        pick(kcat, K, s)
        n, keys = length[s], kcat[s]

        def first_pass(h, _, s=s, n=n, keys=keys):
            q = stacked(qbuf, s, h * HALF * HD, HALF)
            scores = dot(keys, q, ((1,), (1,))) * SCALE
            u = lax.broadcasted_iota(jnp.int32, (LR, WIDE), 0)
            at = lax.rem(lax.broadcasted_iota(jnp.int32, (LR, WIDE), 1), LR)
            own_scores = jnp.where((u <= at) & (u < n), scores[PL:], -jnp.inf)
            scores = jnp.concatenate([scores[:PL], own_scores], axis=0)
            top = jnp.max(scores, axis=0, keepdims=True)
            e = jnp.exp(scores - top)
            probs = e * (1.0 / jnp.sum(e, axis=0, keepdims=True))
            cols = columns(WIDE, h)
            probs_f[s, :, cols] = probs
            probs_t[s, :, cols] = probs.astype(BF)
            return 0

        lax.fori_loop(0, 2, first_pass, 0)
        hand_over(V, s, dot(probs_t[s], stacked(gbuf, s, 0, GROUP), ((1,), (0,))))

    learner2 = dp + 1 - 2 * core
    slot_prompts = prompt + [lax.div(lists[s, learner2], G) for s in range(SLOTS)]

    def fill(kv, first, count):
        def one(i, _):
            k = lax.rem(first + i, Z)
            for a in range(2):
                code = owners[(y + a - 2 * a * y) * (2 * Z) + lax.rem(z + k + 8, Z) * 2 + core]
                p, b = lax.div(code, BLOCKS), lax.rem(code, BLOCKS)
                total = jnp.zeros((BR, HD), F32)
                for c in range(2):
                    for s in range(SLOTS):
                        hit = slot_prompts[c * SLOTS + s] == p
                        total = total + jnp.where(hit, compact[kv][c, s, b].astype(F32), 0.0)
                part[kv, k, a] = total.astype(BF)
            return 0

        lax.fori_loop(0, count, one, 0)

    def set_out(kv):
        wait(compact[kv].at[1], cc_r.at[kv])
        fill(kv, 13, 4)
        for i, d in enumerate((4, 3, 2, 1)):
            send(part.at[kv, (8 + d + 4) % Z], relay_a.at[kv, i], rs_s.at[0], rs_r.at[kv, 0], at_z(d))
        fill(kv, 1, 3)
        for i, d in enumerate((-3, -2, -1)):
            send(part.at[kv, 8 + d - 4], relay_b.at[kv, i], rs_s.at[0], rs_r.at[kv, 1], at_z(d))
        fill(kv, 4, 9)
        for i, d in enumerate(NEAR[2:]):
            send(part.at[kv, 8 + d], direct.at[kv, i], rs_s.at[0], rs_r.at[kv, 2], at_z(d))

    def relay(kv):
        for j, (slot, buf, count) in enumerate(((12, relay_a, 4), (4, relay_b, 3))):
            wait(buf.at[kv], rs_r.at[kv, j])
            total = part[kv, slot].astype(F32)
            for i in range(count):
                total = total + buf[kv, i].astype(F32)
            part[kv, slot] = total.astype(BF)
            send(part.at[kv, slot], relayed.at[kv, j], rs_s.at[0], rs_r.at[kv, 3], at_z(slot - 8))

    def to_other_y(kv):
        wait(direct.at[kv], rs_r.at[kv, 2])
        total = part[kv, 8].astype(F32)
        for i in range(6):
            total = total + direct[kv, i].astype(F32)
        wait(relayed.at[kv], rs_r.at[kv, 3])
        for i in range(2):
            total = total + relayed[kv, i].astype(F32)
        rsum[kv] = total
        send(rsum.at[kv, 1], ysum.at[kv], fy_s.at[0], fy_r.at[kv], other_y)

    wait(table[V].at[:, 1], agc_r.at[V])
    for s in range(SLOTS):
        pick(vcat, V, s)
        n, keys, values = length[s], kcat[s], vcat[s]

        def second_pass(h, _, s=s, n=n, keys=keys, values=values):
            g = stacked(gbuf, s, h * HALF * HD, HALF)
            cols = columns(WIDE, h)
            rounded = probs_t[s, :, cols]
            dprob = dot(values, g, ((1,), (1,)))
            delta = jnp.sum(rounded.astype(F32) * dprob, axis=0, keepdims=True)
            dscore = (probs_f[s, :, cols] * (dprob - delta) * SCALE).astype(BF)
            dscore_t[:, cols] = dscore
            out = dot(rounded, values, ((0,), (0,)))
            dq = dot(dscore, keys, ((0,), (0,)))
            live = lax.broadcasted_iota(jnp.int32, (LR, HD), 0) < n
            for i in range(HALF):
                head = pl.ds(pl.multiple_of(h * HALF * HD + i * HD, HD), HD)
                rows = slice(i * LR, (i + 1) * LR)
                obuf[4 * s : 4 * s + 4, :, head] = jnp.where(live, out[rows], 0.0).astype(BF).reshape(4, 16, HD)
                dqbuf[4 * s : 4 * s + 4, :, head] = dq[rows].astype(BF).reshape(4, 16, HD)
            return 0

        lax.fori_loop(0, 2, second_pass, 0)
        hand_over(K, s, dot(dscore_t[...], stacked(qbuf, s, 0, GROUP), ((1,), (0,))))
        if s == 0:
            set_out(V)

    set_out(K)
    relay(V)

    results = ((obuf, att_out, HW), (dqbuf, qg_out, HW), (rgbuf, rg_out, KW))
    for a, (src, to, width) in enumerate(results):
        for p in peers:
            send(src.at[p], to.at[:, columns(width, t)], back_s.at[a], back_r.at[a], (dp, p))
    stay = [
        pltpu.make_async_copy(src.at[t], to.at[:, columns(width, t)], loc.at[a])
        for a, (src, to, width) in enumerate(results)
    ]
    for copy in stay:
        copy.start()

    relay(K)
    to_other_y(V)
    to_other_y(K)
    for kv in (V, K):
        wait(ysum.at[kv], fy_r.at[kv])
        pg_out[:, kv * HD : (kv + 1) * HD] = (rsum[kv, 0] + ysum[kv]).astype(BF)

    for a, (buf, _, _) in enumerate(results):
        wait(buf.at[pl.ds(0, T - 1)], back_r.at[a])
        wait(buf.at[pl.ds(0, T - 1)], back_s.at[a])
    for copy in stay:
        copy.wait()
    for a, buf in enumerate((kvbuf, qbuf, gbuf)):
        wait(buf.at[pl.ds(0, T - 1)], a2a_s.at[a])
    for kv in (K, V):
        wait(table[kv].at[0, 0, pl.ds(0, 15)], agz_s.at[kv])
        wait(table[kv].at[0, 0], agy_s.at[kv])
        wait(table[kv].at[:, 0], agc_s.at[kv])
        wait(compact[kv].at[0], cc_s.at[kv])
    wait(part.at[:, pl.ds(0, 15)], rs_s.at[0])
    wait(ysum, fy_s.at[0])


def hand_on(*refs):
    sem = refs[8]
    copies = [pltpu.make_async_copy(refs[i], refs[4 + i], sem.at[i]) for i in range(4)]
    for copy in copies:
        copy.start()
    for copy in copies:
        copy.wait()


def on_device(resp_q, resp_kv, prompt_kv, grad_out, lengths, resp_lists, owner_map):
    anywhere = pl.BlockSpec(memory_space=pl.ANY)
    in_vmem = pl.BlockSpec(memory_space=pltpu.VMEM)
    rows = resp_q.shape[0]
    dma = pltpu.SemaphoreType.DMA
    results = pl.pallas_call(
        kernel,
        name="attention",
        out_shape=(
            jax.ShapeDtypeStruct(resp_q.shape, BF),
            jax.ShapeDtypeStruct(resp_q.shape, BF),
            jax.ShapeDtypeStruct(resp_kv.shape, BF),
            jax.ShapeDtypeStruct(prompt_kv.shape, BF),
        ),
        in_specs=[anywhere] * 7,
        out_specs=(anywhere, anywhere, anywhere, in_vmem),
        scratch_shapes=[
            pltpu.VMEM((T, rows, HW), BF),
            pltpu.VMEM((T, rows, HW), BF),
            pltpu.VMEM((T, rows, KW), BF),
            pltpu.VMEM((T, rows, HW), BF),
            pltpu.VMEM((T, rows, HW), BF),
            pltpu.VMEM((T, rows, KW), BF),
            pltpu.VMEM((2, 2, Z, BR, HD), BF),
            pltpu.VMEM((2, 2, Z, BR, HD), BF),
            pltpu.VMEM((SLOTS, KEYS, HD), BF),
            pltpu.VMEM((SLOTS, KEYS, HD), BF),
            pltpu.VMEM((SLOTS, KEYS, GROUP * LR), F32),
            pltpu.VMEM((SLOTS, KEYS, GROUP * LR), BF),
            pltpu.VMEM((KEYS, GROUP * LR), BF),
            pltpu.VMEM((2, SLOTS, BLOCKS, BR, HD), BF),
            pltpu.VMEM((2, SLOTS, BLOCKS, BR, HD), BF),
            pltpu.VMEM((2, Z, 2, BR, HD), BF),
            pltpu.VMEM((2, 6, 2, BR, HD), BF),
            pltpu.VMEM((2, 4, 2, BR, HD), BF),
            pltpu.VMEM((2, 3, 2, BR, HD), BF),
            pltpu.VMEM((2, 2, 2, BR, HD), BF),
            pltpu.VMEM((2, 2, BR, HD), F32),
            pltpu.VMEM((2, BR, HD), F32),
            pltpu.SMEM(lengths.shape, jnp.int32),
            pltpu.SMEM(resp_lists.shape[::-1], jnp.int32),
            pltpu.SMEM(owner_map.shape, jnp.int32),
            dma((8,)),
            dma((3,)),
            dma((3,)),
            dma((2,)),
            dma((2, 5)),
            dma((2,)),
            dma((2, 3)),
            dma((2,)),
            dma((2,)),
            dma((3,)),
            dma((3,)),
            dma((2,)),
            dma((2,)),
            dma((1,)),
            dma((2, 4)),
            dma((1,)),
            dma((2,)),
        ],
        compiler_params=pltpu.CompilerParams(
            collective_id=0, has_side_effects=True, vmem_limit_bytes=60 * 1024 * 1024
        ),
    )(resp_q, resp_kv, prompt_kv, grad_out, lengths, resp_lists.T, owner_map)
    return pl.pallas_call(
        hand_on,
        name="hand_on",
        out_shape=tuple(jax.ShapeDtypeStruct(r.shape, r.dtype) for r in results),
        in_specs=[in_vmem] * 4,
        out_specs=(anywhere,) * 4,
        scratch_shapes=[dma((4,))],
    )(*results)


def solution(mesh):
    rows = P(("dp", "tensor"), None)
    return jax.shard_map(
        on_device,
        mesh=mesh,
        in_specs=(rows, rows, P("dp", "tensor"), rows, P(), P(), P()),
        out_specs=(rows, rows, rows, P("dp", "tensor")),
        check_vma=False,
    )
```

time: 64.5 us -> 56.1 us (0.87)
  local copies, waits for them, and re-layouts: 6.17 us -> 0 us
  Pallas kernels: 57.4 us -> 55.2 us
    unnamed x17 -> x0, local copies, waits for them, and re-layouts: 6.17 us -> none
    pallas_call x1, Pallas kernels: 57.4 us -> 53.4 us  [on_device(): pl.pallas_call(kernel, name='attention', out_shape=(jax.ShapeDtypeStruct(...]
    pallas_call x0 -> x1, Pallas kernels: none -> 1.87 us  [on_device(): pl.pallas_call(hand_on, name='hand_on', out_shape=tuple((jax.ShapeDtypeSt...]
where the time goes in v2:
time: 56.1 us; the launch traced here: 55.9 us
  Pallas kernels  55.2 us (98%)
  between operations  0.64 us (1%)
    pallas_call x1, Pallas kernels, on_device(): pl.pallas_call(kernel, name='attention', out_shape=(jax.ShapeDtypeStruct(...  53.4 us
    pallas_call x1, Pallas kernels, on_device(): pl.pallas_call(hand_on, name='hand_on', out_shape=tuple((jax.ShapeDtypeSt...  1.87 us

profile of v2, /device:TPU:8, one launch (start us, length us, event | category | flops | bytes accessed | tf_op | source)
XLA Modules:
  0.0 55.9 jit_solution(3023837014455268953)
XLA Ops:
  0.6 53.4 %attention.1 = (bf16[16,8192]{1,0:T(8,128)(2,1)}, bf16[16,8192]{1,0:T(8,128)(2,1)}, bf16[16,2048]{1,0:T(8,128)(2,1)}, bf16[32,256]{1,0:T(8,128)(2,1)}) custom-call(bf16[16,8192]{1,0:T(8,128)(2,1)} %q_in.1, bf16[16,2048]{1,0:T(8,128)(2,1)} %kv_in.1, bf16[32,256]{1,0:T(8,128)(2,1)} %pkv_in.1, bf16[16,8192]{1,0:T(8,128)(2,1)} %g_in.1, s32[128]{0:T(128)} %lengths_in.1, ...), custom_call_target="tpu_custom_call" | custom-call | tf_op jit(solution)/shard_map/attention/pallas_call | solution.py:339
  54.0 1.9 %hand_on.1 = (bf16[16,8192]{1,0:T(8,128)(2,1)}, bf16[16,8192]{1,0:T(8,128)(2,1)}, bf16[16,2048]{1,0:T(8,128)(2,1)}, bf16[32,256]{1,0:T(8,128)(2,1)}) custom-call(bf16[16,8192]{1,0:T(8,128)(2,1)} %get-tuple-element.8.refs_0_, bf16[16,8192]{1,0:T(8,128)(2,1)} %get-tuple-element.9.refs_1_, bf16[16,2048]{1,0:T(8,128)(2,1)} %get-tuple-element.10.refs_2_, ...), custom_call_target="tpu_custom_call" | custom-call | tf_op jit(solution)/shard_map/hand_on/pallas_call | solution.py:398

commit v3 on v2

--- a/solution.py
+++ b/solution.py
@@ -27,6 +27,7 @@
 WIDE = HALF * LR
 SCALE = 1.0 / math.sqrt(HD)
 NEAR = (4, -4, 3, -3, 2, -2, 1, -1)
+DIRECT = tuple((a, d) for d in NEAR[2:] for a in (1, 0)) + ((1, 0),)
 K, V = 0, 1
 
 
@@ -39,8 +40,8 @@
     att_out, qg_out, rg_out, pg_out,
     qbuf, gbuf, kvbuf, obuf, dqbuf, rgbuf,
     table_k, table_v, kcat, vcat, probs_f, probs_t, dscore_t,
-    compact_k, compact_v, part, direct, relay_a, relay_b, relayed, rsum, ysum, lengths, lists, owners,
-    loc, a2a_s, a2a_r, agz_s, agz_r, agy_s, agy_r, agc_s, agc_r, back_s, back_r, cc_s, cc_r, rs_s, rs_r, fy_s, fy_r,
+    compact_k, compact_v, part, direct, relay_a, relay_b, relayed, lengths, lists, owners,
+    loc, a2a_s, a2a_r, agz_s, agz_r, agy_s, agy_r, agc_s, agc_r, back_s, back_r, cc_s, cc_r, rs_s, rs_r,
 ):
     table, compact = (table_k, table_v), (compact_k, compact_v)
     dp = lax.axis_index("dp")
@@ -49,11 +50,10 @@
     z = lax.rem(dp // 2, Z)
     y = dp // (2 * Z)
 
-    def at_z(d):
-        return (y * (2 * Z) + lax.rem(z + d + Z, Z) * 2 + core, t)
+    def at(a, d):
+        return ((y + a - 2 * a * y) * (2 * Z) + lax.rem(z + d + Z, Z) * 2 + core, t)
 
     other_core = (y * (2 * Z) + z * 2 + (1 - core), t)
-    other_y = ((1 - y) * (2 * Z) + z * 2 + core, t)
     peers = [lax.rem(t + k, T) for k in range(1, T)]
 
     def send(src, dst, s, r, device):
@@ -68,7 +68,7 @@
         return pl.ds(pl.multiple_of(index * width, width), width)
 
     barrier = pltpu.get_barrier_semaphore()
-    greeted = [(dp, p) for p in peers] + [at_z(d) for d in NEAR] + [other_y, other_core]
+    greeted = [(dp, p) for p in peers] + [at(a, d) for d in NEAR for a in (1, 0)] + [at(1, 0), other_core]
     for device in greeted:
         pl.semaphore_signal(barrier, inc=1, device_id=device, device_id_type=MESH)
     local = [
@@ -87,38 +87,36 @@
         copy.wait()
     pl.semaphore_wait(barrier, len(greeted))
 
-    def arrival(slot):
-        return 0 if slot == 4 else 1 if slot == 12 else 2 if 4 < slot < 12 else 3 if slot < 4 else 4
-
-    def gather(kv, slot, d):
+    def arrival(a, slot):
+        return 0 if slot == 4 else 1 if slot == 12 else 2 if 4 < slot < 12 else 3 + 2 * a if slot < 4 else 4 + 2 * a
+
+    def gather(kv, a, slot, d):
         to = slot - d
-        send(table[kv].at[0, 0, slot], table[kv].at[0, 0, to], agz_s.at[kv], agz_r.at[kv, arrival(to)], at_z(d))
+        send(table[kv].at[0, 0, slot], table[kv].at[a, 0, to], agz_s.at[kv], agz_r.at[kv, arrival(a, to)], at(a, d))
 
     def to_heads(a, src, dst, width):
         for p in peers:
             send(src.at[:, columns(width, p)], dst.at[t], a2a_s.at[a], a2a_r.at[a], (dp, p))
 
     for d in NEAR:
-        gather(K, 8, d)
+        gather(K, 0, 8, d)
     to_heads(0, kv_in, kvbuf, KW)
     for d in NEAR:
-        gather(V, 8, d)
+        gather(V, 0, 8, d)
     to_heads(1, q_in, qbuf, HW)
     to_heads(2, g_in, gbuf, HW)
 
     for kv in (K, V):
         wait(table[kv].at[0, 0, 4], agz_r.at[kv, 0])
         for d in (4, 3, 2, 1):
-            gather(kv, 4, d)
+            for a in (1, 0):
+                gather(kv, a, 4, d)
         wait(table[kv].at[0, 0, 12], agz_r.at[kv, 1])
         for d in (-3, -2, -1):
-            gather(kv, 12, d)
+            for a in (1, 0):
+                gather(kv, a, 12, d)
 
     groups = (pl.ds(4, 9), pl.ds(0, 4), pl.ds(13, 3))
-
-    def over_y(kv, i):
-        r = groups[i]
-        send(table[kv].at[0, 0, r], table[kv].at[1, 0, r], agy_s.at[kv], agy_r.at[kv, i], other_y)
 
     def over_core(kv, a, i):
         r = groups[i]
@@ -126,7 +124,8 @@
 
     for kv in (K, V):
         wait(table[kv].at[0, 0, pl.ds(4, 6)], agz_r.at[kv, 2])
-        over_y(kv, 0)
+        near = groups[0]
+        send(table[kv].at[0, 0, near], table[kv].at[1, 0, near], agy_s.at[kv], agy_r.at[kv], at(1, 0))
         over_core(kv, 0, 0)
 
     for copy in local[5:]:
@@ -153,14 +152,12 @@
             cat[s, b * BR : (b + 1) * BR] = block
 
     for kv in (K, V):
+        wait(table[kv].at[1, 0, groups[0]], agy_r.at[kv])
+        over_core(kv, 1, 0)
         for i in (1, 2):
-            wait(table[kv].at[0, 0, groups[i]], agz_r.at[kv, 2 + i])
-            over_y(kv, i)
-            over_core(kv, 0, i)
-    for kv in (K, V):
-        for i in range(3):
-            wait(table[kv].at[1, 0, groups[i]], agy_r.at[kv, i])
-            over_core(kv, 1, i)
+            for a in range(2):
+                wait(table[kv].at[a, 0, groups[i]], agz_r.at[kv, 2 + i + 2 * a])
+                over_core(kv, a, i)
     for copy in local[2:5]:
         copy.wait()
     for a, buf in enumerate((kvbuf, qbuf, gbuf)):
@@ -203,7 +200,7 @@
             probs_t[s, :, cols] = probs.astype(BF)
             return 0
 
-        lax.fori_loop(0, 2, first_pass, 0)
+        lax.fori_loop(0, 2, first_pass, 0, unroll=True)
         hand_over(V, s, dot(probs_t[s], stacked(gbuf, s, 0, GROUP), ((1,), (0,))))
 
     learner2 = dp + 1 - 2 * core
@@ -229,13 +226,13 @@
         wait(compact[kv].at[1], cc_r.at[kv])
         fill(kv, 13, 4)
         for i, d in enumerate((4, 3, 2, 1)):
-            send(part.at[kv, (8 + d + 4) % Z], relay_a.at[kv, i], rs_s.at[0], rs_r.at[kv, 0], at_z(d))
+            send(part.at[kv, (8 + d + 4) % Z], relay_a.at[kv, i], rs_s.at[kv, 0], rs_r.at[kv, 0], at(0, d))
         fill(kv, 1, 3)
         for i, d in enumerate((-3, -2, -1)):
-            send(part.at[kv, 8 + d - 4], relay_b.at[kv, i], rs_s.at[0], rs_r.at[kv, 1], at_z(d))
+            send(part.at[kv, 8 + d - 4], relay_b.at[kv, i], rs_s.at[kv, 0], rs_r.at[kv, 1], at(0, d))
         fill(kv, 4, 9)
-        for i, d in enumerate(NEAR[2:]):
-            send(part.at[kv, 8 + d], direct.at[kv, i], rs_s.at[0], rs_r.at[kv, 2], at_z(d))
+        for i, (a, d) in enumerate(DIRECT):
+            send(part.at[kv, 8 + d, a], direct.at[kv, i], rs_s.at[kv, 1], rs_r.at[kv, 2], at(a, d))
 
     def relay(kv):
         for j, (slot, buf, count) in enumerate(((12, relay_a, 4), (4, relay_b, 3))):
@@ -244,18 +241,18 @@
             for i in range(count):
                 total = total + buf[kv, i].astype(F32)
             part[kv, slot] = total.astype(BF)
-            send(part.at[kv, slot], relayed.at[kv, j], rs_s.at[0], rs_r.at[kv, 3], at_z(slot - 8))
-
-    def to_other_y(kv):
+            for a in (1, 0):
+                send(part.at[kv, slot, a], relayed.at[kv, 2 * j + a], rs_s.at[kv, 2], rs_r.at[kv, 3], at(a, slot - 8))
+
+    def finish(kv):
         wait(direct.at[kv], rs_r.at[kv, 2])
-        total = part[kv, 8].astype(F32)
-        for i in range(6):
+        total = part[kv, 8, 0].astype(F32)
+        for i in range(len(DIRECT)):
             total = total + direct[kv, i].astype(F32)
         wait(relayed.at[kv], rs_r.at[kv, 3])
-        for i in range(2):
+        for i in range(4):
             total = total + relayed[kv, i].astype(F32)
-        rsum[kv] = total
-        send(rsum.at[kv, 1], ysum.at[kv], fy_s.at[0], fy_r.at[kv], other_y)
+        pg_out[:, kv * HD : (kv + 1) * HD] = total.astype(BF)
 
     wait(table[V].at[:, 1], agc_r.at[V])
     for s in range(SLOTS):
@@ -280,7 +277,7 @@
                 dqbuf[4 * s : 4 * s + 4, :, head] = dq[rows].astype(BF).reshape(4, 16, HD)
             return 0
 
-        lax.fori_loop(0, 2, second_pass, 0)
+        lax.fori_loop(0, 2, second_pass, 0, unroll=True)
         hand_over(K, s, dot(dscore_t[...], stacked(qbuf, s, 0, GROUP), ((1,), (0,))))
         if s == 0:
             set_out(V)
@@ -300,11 +297,8 @@
         copy.start()
 
     relay(K)
-    to_other_y(V)
-    to_other_y(K)
-    for kv in (V, K):
-        wait(ysum.at[kv], fy_r.at[kv])
-        pg_out[:, kv * HD : (kv + 1) * HD] = (rsum[kv, 0] + ysum[kv]).astype(BF)
+    finish(V)
+    finish(K)
 
     for a, (buf, _, _) in enumerate(results):
         wait(buf.at[pl.ds(0, T - 1)], back_r.at[a])
@@ -314,12 +308,13 @@
     for a, buf in enumerate((kvbuf, qbuf, gbuf)):
         wait(buf.at[pl.ds(0, T - 1)], a2a_s.at[a])
     for kv in (K, V):
-        wait(table[kv].at[0, 0, pl.ds(0, 15)], agz_s.at[kv])
-        wait(table[kv].at[0, 0], agy_s.at[kv])
+        wait(table[kv].at[:, 0, pl.ds(0, 11)], agz_s.at[kv])
+        wait(table[kv].at[0, 0, near], agy_s.at[kv])
         wait(table[kv].at[:, 0], agc_s.at[kv])
         wait(compact[kv].at[0], cc_s.at[kv])
-    wait(part.at[:, pl.ds(0, 15)], rs_s.at[0])
-    wait(ysum, fy_s.at[0])
+        wait(part.at[kv, pl.ds(0, 7)], rs_s.at[kv, 0])
+        wait(direct.at[kv], rs_s.at[kv, 1])
+        wait(relayed.at[kv], rs_s.at[kv, 2])
 
 
 def hand_on(*refs):
@@ -364,12 +359,10 @@
             pltpu.VMEM((2, SLOTS, BLOCKS, BR, HD), BF),
             pltpu.VMEM((2, SLOTS, BLOCKS, BR, HD), BF),
             pltpu.VMEM((2, Z, 2, BR, HD), BF),
-            pltpu.VMEM((2, 6, 2, BR, HD), BF),
+            pltpu.VMEM((2, len(DIRECT), BR, HD), BF),
             pltpu.VMEM((2, 4, 2, BR, HD), BF),
             pltpu.VMEM((2, 3, 2, BR, HD), BF),
-            pltpu.VMEM((2, 2, 2, BR, HD), BF),
-            pltpu.VMEM((2, 2, BR, HD), F32),
-            pltpu.VMEM((2, BR, HD), F32),
+            pltpu.VMEM((2, 4, BR, HD), BF),
             pltpu.SMEM(lengths.shape, jnp.int32),
             pltpu.SMEM(resp_lists.shape[::-1], jnp.int32),
             pltpu.SMEM(owner_map.shape, jnp.int32),
@@ -377,19 +370,17 @@
             dma((3,)),
             dma((3,)),
             dma((2,)),
-            dma((2, 5)),
-            dma((2,)),
-            dma((2, 3)),
+            dma((2, 7)),
+            dma((2,)),
+            dma((2,)),
             dma((2,)),
             dma((2,)),
             dma((3,)),
             dma((3,)),
             dma((2,)),
             dma((2,)),
-            dma((1,)),
+            dma((2, 3)),
             dma((2, 4)),
-            dma((1,)),
-            dma((2,)),
         ],
         compiler_params=pltpu.CompilerParams(
             collective_id=0, has_side_effects=True, vmem_limit_bytes=60 * 1024 * 1024

time: 56.1 us -> 52.2 us (0.930)
  the two profiles are of different devices: /device:TPU:8 before, /device:TPU:1 now
where the time goes in v3:
time: 52.2 us; the launch traced here: 51.9 us
  Pallas kernels  51.3 us (98%)
  between operations  0.64 us (1%)
    pallas_call x1, Pallas kernels, on_device(): pl.pallas_call(kernel, name='attention', out_shape=(jax.ShapeDtypeStruct(...  49.4 us
    pallas_call x1, Pallas kernels, on_device(): pl.pallas_call(hand_on, name='hand_on', out_shape=tuple((jax.ShapeDtypeSt...  1.87 us

profile of v3, /device:TPU:1, one launch (start us, length us, event | category | flops | bytes accessed | tf_op | source)
XLA Modules:
  0.0 51.9 jit_solution(18000971160103725120)
XLA Ops:
  0.6 49.4 %attention.1 = (bf16[16,8192]{1,0:T(8,128)(2,1)}, bf16[16,8192]{1,0:T(8,128)(2,1)}, bf16[16,2048]{1,0:T(8,128)(2,1)}, bf16[32,256]{1,0:T(8,128)(2,1)}) custom-call(bf16[16,8192]{1,0:T(8,128)(2,1)} %q_in.1, bf16[16,2048]{1,0:T(8,128)(2,1)} %kv_in.1, bf16[32,256]{1,0:T(8,128)(2,1)} %pkv_in.1, bf16[16,8192]{1,0:T(8,128)(2,1)} %g_in.1, s32[128]{0:T(128)} %lengths_in.1, ...), custom_call_target="tpu_custom_call" | custom-call | tf_op jit(solution)/shard_map/attention/pallas_call | solution.py:334
  50.1 1.9 %hand_on.1 = (bf16[16,8192]{1,0:T(8,128)(2,1)}, bf16[16,8192]{1,0:T(8,128)(2,1)}, bf16[16,2048]{1,0:T(8,128)(2,1)}, bf16[32,256]{1,0:T(8,128)(2,1)}) custom-call(bf16[16,8192]{1,0:T(8,128)(2,1)} %get-tuple-element.8.refs_0_, bf16[16,8192]{1,0:T(8,128)(2,1)} %get-tuple-element.9.refs_1_, bf16[16,2048]{1,0:T(8,128)(2,1)} %get-tuple-element.10.refs_2_, ...), custom_call_target="tpu_custom_call" | custom-call | tf_op jit(solution)/shard_map/hand_on/pallas_call | solution.py:389

commit v4 on v3

--- a/solution.py
+++ b/solution.py
@@ -27,7 +27,6 @@
 WIDE = HALF * LR
 SCALE = 1.0 / math.sqrt(HD)
 NEAR = (4, -4, 3, -3, 2, -2, 1, -1)
-DIRECT = tuple((a, d) for d in NEAR[2:] for a in (1, 0)) + ((1, 0),)
 K, V = 0, 1
 
 
@@ -40,7 +39,7 @@
     att_out, qg_out, rg_out, pg_out,
     qbuf, gbuf, kvbuf, obuf, dqbuf, rgbuf,
     table_k, table_v, kcat, vcat, probs_f, probs_t, dscore_t,
-    compact_k, compact_v, part, direct, relay_a, relay_b, relayed, lengths, lists, owners,
+    compact_k, compact_v, part, direct, relay_a, relay_b, relayed, ypart, lengths, lists, owners,
     loc, a2a_s, a2a_r, agz_s, agz_r, agy_s, agy_r, agc_s, agc_r, back_s, back_r, cc_s, cc_r, rs_s, rs_r,
 ):
     table, compact = (table_k, table_v), (compact_k, compact_v)
@@ -50,8 +49,10 @@
     z = lax.rem(dp // 2, Z)
     y = dp // (2 * Z)
 
+    way = 1 - 2 * core
+
     def at(a, d):
-        return ((y + a - 2 * a * y) * (2 * Z) + lax.rem(z + d + Z, Z) * 2 + core, t)
+        return ((y + a - 2 * a * y) * (2 * Z) + lax.rem(z + way * d + Z, Z) * 2 + core, t)
 
     other_core = (y * (2 * Z) + z * 2 + (1 - core), t)
     peers = [lax.rem(t + k, T) for k in range(1, T)]
@@ -100,9 +101,9 @@
 
     for d in NEAR:
         gather(K, 0, 8, d)
-    to_heads(0, kv_in, kvbuf, KW)
     for d in NEAR:
         gather(V, 0, 8, d)
+    to_heads(0, kv_in, kvbuf, KW)
     to_heads(1, q_in, qbuf, HW)
     to_heads(2, g_in, gbuf, HW)
 
@@ -148,7 +149,8 @@
         for b in range(BLOCKS):
             j = found[s * BLOCKS + b]
             jy, jz, jc = lax.div(j, 2 * Z), lax.rem(lax.div(j, 2), Z), lax.rem(j, 2)
-            block = table[kv][jnp.where(jy == y, 0, 1), jnp.where(jc == core, 0, 1), lax.rem(jz - z + 8 + Z, Z)]
+            slot = lax.rem((1 - 2 * jc) * (jz - z) + 8 + Z, Z)
+            block = table[kv][jnp.where(jy == y, 0, 1), jnp.where(jc == core, 0, 1), slot]
             cat[s, b * BR : (b + 1) * BR] = block
 
     for kv in (K, V):
@@ -210,46 +212,55 @@
         def one(i, _):
             k = lax.rem(first + i, Z)
             for a in range(2):
-                code = owners[(y + a - 2 * a * y) * (2 * Z) + lax.rem(z + k + 8, Z) * 2 + core]
+                code = owners[(y + a - 2 * a * y) * (2 * Z) + lax.rem(z + way * (k - 8) + Z, Z) * 2 + core]
                 p, b = lax.div(code, BLOCKS), lax.rem(code, BLOCKS)
                 total = jnp.zeros((BR, HD), F32)
                 for c in range(2):
                     for s in range(SLOTS):
                         hit = slot_prompts[c * SLOTS + s] == p
                         total = total + jnp.where(hit, compact[kv][c, s, b].astype(F32), 0.0)
-                part[kv, k, a] = total.astype(BF)
+                part[kv, a, k] = total.astype(BF)
             return 0
 
         lax.fori_loop(0, count, one, 0)
 
-    def set_out(kv):
+    def far(kv):
         wait(compact[kv].at[1], cc_r.at[kv])
         fill(kv, 13, 4)
         for i, d in enumerate((4, 3, 2, 1)):
-            send(part.at[kv, (8 + d + 4) % Z], relay_a.at[kv, i], rs_s.at[kv, 0], rs_r.at[kv, 0], at(0, d))
+            send(part.at[kv, :, (8 + d + 4) % Z], relay_a.at[kv, i], rs_s.at[kv, 0], rs_r.at[kv, 0], at(0, d))
         fill(kv, 1, 3)
         for i, d in enumerate((-3, -2, -1)):
-            send(part.at[kv, 8 + d - 4], relay_b.at[kv, i], rs_s.at[kv, 0], rs_r.at[kv, 1], at(0, d))
+            send(part.at[kv, :, 8 + d - 4], relay_b.at[kv, i], rs_s.at[kv, 0], rs_r.at[kv, 1], at(0, d))
+
+    near_slots = pl.ds(5, 7)
+
+    def near_y(kv):
         fill(kv, 4, 9)
-        for i, (a, d) in enumerate(DIRECT):
-            send(part.at[kv, 8 + d, a], direct.at[kv, i], rs_s.at[kv, 1], rs_r.at[kv, 2], at(a, d))
+        send(part.at[kv, 1, near_slots], ypart.at[kv], rs_s.at[kv, 1], rs_r.at[kv, 2], at(1, 0))
+
+    def near_z(kv):
+        wait(ypart.at[kv], rs_r.at[kv, 2])
+        part[kv, 0, near_slots] = (part[kv, 0, near_slots].astype(F32) + ypart[kv].astype(F32)).astype(BF)
+        for i, d in enumerate(NEAR[2:]):
+            send(part.at[kv, 0, 8 + d], direct.at[kv, i], rs_s.at[kv, 2], rs_r.at[kv, 3], at(0, d))
 
     def relay(kv):
         for j, (slot, buf, count) in enumerate(((12, relay_a, 4), (4, relay_b, 3))):
             wait(buf.at[kv], rs_r.at[kv, j])
-            total = part[kv, slot].astype(F32)
+            total = part[kv, :, slot].astype(F32)
             for i in range(count):
                 total = total + buf[kv, i].astype(F32)
-            part[kv, slot] = total.astype(BF)
+            part[kv, :, slot] = total.astype(BF)
             for a in (1, 0):
-                send(part.at[kv, slot, a], relayed.at[kv, 2 * j + a], rs_s.at[kv, 2], rs_r.at[kv, 3], at(a, slot - 8))
+                send(part.at[kv, a, slot], relayed.at[kv, 2 * j + a], rs_s.at[kv, 3], rs_r.at[kv, 4], at(a, slot - 8))
 
     def finish(kv):
-        wait(direct.at[kv], rs_r.at[kv, 2])
-        total = part[kv, 8, 0].astype(F32)
-        for i in range(len(DIRECT)):
+        wait(direct.at[kv], rs_r.at[kv, 3])
+        total = part[kv, 0, 8].astype(F32)
+        for i in range(6):
             total = total + direct[kv, i].astype(F32)
-        wait(relayed.at[kv], rs_r.at[kv, 3])
+        wait(relayed.at[kv], rs_r.at[kv, 4])
         for i in range(4):
             total = total + relayed[kv, i].astype(F32)
         pg_out[:, kv * HD : (kv + 1) * HD] = total.astype(BF)
@@ -257,46 +268,55 @@
     wait(table[V].at[:, 1], agc_r.at[V])
     for s in range(SLOTS):
         pick(vcat, V, s)
-        n, keys, values = length[s], kcat[s], vcat[s]
-
-        def second_pass(h, _, s=s, n=n, keys=keys, values=values):
+        values = vcat[s]
+
+        def second_pass(h, _, s=s, values=values):
             g = stacked(gbuf, s, h * HALF * HD, HALF)
             cols = columns(WIDE, h)
-            rounded = probs_t[s, :, cols]
             dprob = dot(values, g, ((1,), (1,)))
-            delta = jnp.sum(rounded.astype(F32) * dprob, axis=0, keepdims=True)
-            dscore = (probs_f[s, :, cols] * (dprob - delta) * SCALE).astype(BF)
-            dscore_t[:, cols] = dscore
-            out = dot(rounded, values, ((0,), (0,)))
-            dq = dot(dscore, keys, ((0,), (0,)))
-            live = lax.broadcasted_iota(jnp.int32, (LR, HD), 0) < n
-            for i in range(HALF):
-                head = pl.ds(pl.multiple_of(h * HALF * HD + i * HD, HD), HD)
-                rows = slice(i * LR, (i + 1) * LR)
-                obuf[4 * s : 4 * s + 4, :, head] = jnp.where(live, out[rows], 0.0).astype(BF).reshape(4, 16, HD)
-                dqbuf[4 * s : 4 * s + 4, :, head] = dq[rows].astype(BF).reshape(4, 16, HD)
+            delta = jnp.sum(probs_t[s, :, cols].astype(F32) * dprob, axis=0, keepdims=True)
+            dscore_t[s, :, cols] = (probs_f[s, :, cols] * (dprob - delta) * SCALE).astype(BF)
             return 0
 
         lax.fori_loop(0, 2, second_pass, 0, unroll=True)
-        hand_over(K, s, dot(dscore_t[...], stacked(qbuf, s, 0, GROUP), ((1,), (0,))))
+        hand_over(K, s, dot(dscore_t[s], stacked(qbuf, s, 0, GROUP), ((1,), (0,))))
         if s == 0:
-            set_out(V)
-
-    set_out(K)
-    relay(V)
+            far(V)
 
     results = ((obuf, att_out, HW), (dqbuf, qg_out, HW), (rgbuf, rg_out, KW))
-    for a, (src, to, width) in enumerate(results):
+
+    def to_rows(a):
+        src, to, width = results[a]
         for p in peers:
             send(src.at[p], to.at[:, columns(width, t)], back_s.at[a], back_r.at[a], (dp, p))
-    stay = [
-        pltpu.make_async_copy(src.at[t], to.at[:, columns(width, t)], loc.at[a])
-        for a, (src, to, width) in enumerate(results)
-    ]
-    for copy in stay:
+        copy = pltpu.make_async_copy(src.at[t], to.at[:, columns(width, t)], loc.at[a])
         copy.start()
-
+        return copy
+
+    def back(a, left, right):
+        for s in range(SLOTS):
+            for h in range(2):
+                rows = dot(left[s, :, h * WIDE : (h + 1) * WIDE], right[s], ((0,), (0,)))
+                for i in range(HALF):
+                    head = slice((h * HALF + i) * HD, (h * HALF + i + 1) * HD)
+                    values = rows[i * LR : (i + 1) * LR]
+                    if a == 0:
+                        live = lax.broadcasted_iota(jnp.int32, (LR, HD), 0) < length[s]
+                        values = jnp.where(live, values, 0.0)
+                    results[a][0][4 * s : 4 * s + 4, :, head] = values.astype(BF).reshape(4, 16, HD)
+
+    far(K)
+    near_y(V)
+    near_y(K)
+    back(0, probs_t, vcat)
+    near_z(V)
+    near_z(K)
+    stay = [to_rows(0)]
+    relay(V)
+    back(1, dscore_t, kcat)
     relay(K)
+    stay.append(to_rows(2))
+    stay.append(to_rows(1))
     finish(V)
     finish(K)
 
@@ -312,18 +332,25 @@
         wait(table[kv].at[0, 0, near], agy_s.at[kv])
         wait(table[kv].at[:, 0], agc_s.at[kv])
         wait(compact[kv].at[0], cc_s.at[kv])
-        wait(part.at[kv, pl.ds(0, 7)], rs_s.at[kv, 0])
-        wait(direct.at[kv], rs_s.at[kv, 1])
-        wait(relayed.at[kv], rs_s.at[kv, 2])
+        wait(part.at[kv, :, pl.ds(0, 7)], rs_s.at[kv, 0])
+        wait(ypart.at[kv], rs_s.at[kv, 1])
+        wait(direct.at[kv], rs_s.at[kv, 2])
+        wait(relayed.at[kv], rs_s.at[kv, 3])
 
 
 def hand_on(*refs):
-    sem = refs[8]
-    copies = [pltpu.make_async_copy(refs[i], refs[4 + i], sem.at[i]) for i in range(4)]
-    for copy in copies:
-        copy.start()
-    for copy in copies:
-        copy.wait()
+    held, sem = refs[8:12], refs[12]
+    copies = [
+        (pltpu.make_async_copy(refs[i], held[i], sem.at[i]), pltpu.make_async_copy(held[i], refs[4 + i], sem.at[i]))
+        for i in range(4)
+    ]
+    for first, _ in copies:
+        first.start()
+    for first, second in copies:
+        first.wait()
+        second.start()
+    for _, second in copies:
+        second.wait()
 
 
 def on_device(resp_q, resp_kv, prompt_kv, grad_out, lengths, resp_lists, owner_map):
@@ -355,14 +382,15 @@
             pltpu.VMEM((SLOTS, KEYS, HD), BF),
             pltpu.VMEM((SLOTS, KEYS, GROUP * LR), F32),
             pltpu.VMEM((SLOTS, KEYS, GROUP * LR), BF),
-            pltpu.VMEM((KEYS, GROUP * LR), BF),
+            pltpu.VMEM((SLOTS, KEYS, GROUP * LR), BF),
             pltpu.VMEM((2, SLOTS, BLOCKS, BR, HD), BF),
             pltpu.VMEM((2, SLOTS, BLOCKS, BR, HD), BF),
-            pltpu.VMEM((2, Z, 2, BR, HD), BF),
-            pltpu.VMEM((2, len(DIRECT), BR, HD), BF),
+            pltpu.VMEM((2, 2, Z, BR, HD), BF),
+            pltpu.VMEM((2, 6, BR, HD), BF),
             pltpu.VMEM((2, 4, 2, BR, HD), BF),
             pltpu.VMEM((2, 3, 2, BR, HD), BF),
             pltpu.VMEM((2, 4, BR, HD), BF),
+            pltpu.VMEM((2, 7, BR, HD), BF),
             pltpu.SMEM(lengths.shape, jnp.int32),
             pltpu.SMEM(resp_lists.shape[::-1], jnp.int32),
             pltpu.SMEM(owner_map.shape, jnp.int32),
@@ -379,8 +407,8 @@
             dma((3,)),
             dma((2,)),
             dma((2,)),
-            dma((2, 3)),
             dma((2, 4)),
+            dma((2, 5)),
         ],
         compiler_params=pltpu.CompilerParams(
             collective_id=0, has_side_effects=True, vmem_limit_bytes=60 * 1024 * 1024
@@ -390,9 +418,10 @@
         hand_on,
         name="hand_on",
         out_shape=tuple(jax.ShapeDtypeStruct(r.shape, r.dtype) for r in results),
-        in_specs=[in_vmem] * 4,
+        in_specs=[anywhere] * 4,
         out_specs=(anywhere,) * 4,
-        scratch_shapes=[dma((4,))],
+        scratch_shapes=[pltpu.VMEM(r.shape, r.dtype) for r in results] + [dma((4,))],
+        compiler_params=pltpu.CompilerParams(vmem_limit_bytes=60 * 1024 * 1024),
     )(*results)
 
 

time: 52.2 us -> 51 us (0.977)
  Pallas kernels: 51.3 us -> 50.2 us
    pallas_call x1, Pallas kernels: 49.4 us -> 48.4 us  [on_device(): pl.pallas_call(kernel, name='attention', out_shape=(jax.ShapeDtypeStruct(...]
where the time goes in v4:
time: 51 us; the launch traced here: 50.8 us
  Pallas kernels  50.2 us (98%)
  between operations  0.64 us (1%)
    pallas_call x1, Pallas kernels, on_device(): pl.pallas_call(kernel, name='attention', out_shape=(jax.ShapeDtypeStruct(...  48.4 us
    pallas_call x1, Pallas kernels, on_device(): pl.pallas_call(hand_on, name='hand_on', out_shape=tuple((jax.ShapeDtypeSt...  1.79 us

profile of v4, /device:TPU:1, one launch (start us, length us, event | category | flops | bytes accessed | tf_op | source)
XLA Modules:
  0.0 50.8 jit_solution(17032203489160334930)
XLA Ops:
  0.6 48.4 %attention.1 = (bf16[16,8192]{1,0:T(8,128)(2,1)}, bf16[16,8192]{1,0:T(8,128)(2,1)}, bf16[16,2048]{1,0:T(8,128)(2,1)}, bf16[32,256]{1,0:T(8,128)(2,1)}) custom-call(bf16[16,8192]{1,0:T(8,128)(2,1)} %q_in.1, bf16[16,2048]{1,0:T(8,128)(2,1)} %kv_in.1, bf16[32,256]{1,0:T(8,128)(2,1)} %pkv_in.1, bf16[16,8192]{1,0:T(8,128)(2,1)} %g_in.1, s32[128]{0:T(128)} %lengths_in.1, ...), custom_call_target="tpu_custom_call" | custom-call | tf_op jit(solution)/shard_map/attention/pallas_call | solution.py:361
  49.0 1.8 %hand_on.1 = (bf16[16,8192]{1,0:T(8,128)(2,1)}, bf16[16,8192]{1,0:T(8,128)(2,1)}, bf16[16,2048]{1,0:T(8,128)(2,1)}, bf16[32,256]{1,0:T(8,128)(2,1)}) custom-call(bf16[16,8192]{1,0:T(8,128)(2,1)} %get-tuple-element.8.refs_0_, bf16[16,8192]{1,0:T(8,128)(2,1)} %get-tuple-element.9.refs_1_, bf16[16,2048]{1,0:T(8,128)(2,1)} %get-tuple-element.10.refs_2_, ...), custom_call_target="tpu_custom_call" | custom-call | tf_op jit(solution)/shard_map/hand_on/pallas_call | solution.py:417

commit v5 on v4

--- a/solution.py
+++ b/solution.py
@@ -40,7 +40,7 @@
     qbuf, gbuf, kvbuf, obuf, dqbuf, rgbuf,
     table_k, table_v, kcat, vcat, probs_f, probs_t, dscore_t,
     compact_k, compact_v, part, direct, relay_a, relay_b, relayed, ypart, lengths, lists, owners,
-    loc, a2a_s, a2a_r, agz_s, agz_r, agy_s, agy_r, agc_s, agc_r, back_s, back_r, cc_s, cc_r, rs_s, rs_r,
+    loc, a2a_s, a2a_r, agz_s, agz_r, agy_s, agy_r, agc_s, agc_r, back_s, back_r, cc_s, cc_r, rs_s, rs_r, heard,
 ):
     table, compact = (table_k, table_v), (compact_k, compact_v)
     dp = lax.axis_index("dp")
@@ -69,7 +69,7 @@
         return pl.ds(pl.multiple_of(index * width, width), width)
 
     barrier = pltpu.get_barrier_semaphore()
-    greeted = [(dp, p) for p in peers] + [at(a, d) for d in NEAR for a in (1, 0)] + [at(1, 0), other_core]
+    greeted = [(dp, p) for p in peers] + [at(0, d) for d in NEAR] + [at(1, 0), other_core]
     for device in greeted:
         pl.semaphore_signal(barrier, inc=1, device_id=device, device_id_type=MESH)
     local = [
@@ -87,6 +87,7 @@
     for copy in local[:2]:
         copy.wait()
     pl.semaphore_wait(barrier, len(greeted))
+    pl.semaphore_signal(heard, inc=1, device_id=at(1, 0), device_id_type=MESH)
 
     def arrival(a, slot):
         return 0 if slot == 4 else 1 if slot == 12 else 2 if 4 < slot < 12 else 3 + 2 * a if slot < 4 else 4 + 2 * a
@@ -107,6 +108,7 @@
     to_heads(1, q_in, qbuf, HW)
     to_heads(2, g_in, gbuf, HW)
 
+    pl.semaphore_wait(heard, 1)
     for kv in (K, V):
         wait(table[kv].at[0, 0, 4], agz_r.at[kv, 0])
         for d in (4, 3, 2, 1):
@@ -222,15 +224,18 @@
                 part[kv, a, k] = total.astype(BF)
             return 0
 
-        lax.fori_loop(0, count, one, 0)
+        if count == 1:
+            one(0, 0)
+        else:
+            lax.fori_loop(0, count, one, 0)
 
     def far(kv):
         wait(compact[kv].at[1], cc_r.at[kv])
-        fill(kv, 13, 4)
         for i, d in enumerate((4, 3, 2, 1)):
+            fill(kv, (8 + d + 4) % Z, 1)
             send(part.at[kv, :, (8 + d + 4) % Z], relay_a.at[kv, i], rs_s.at[kv, 0], rs_r.at[kv, 0], at(0, d))
-        fill(kv, 1, 3)
         for i, d in enumerate((-3, -2, -1)):
+            fill(kv, 8 + d - 4, 1)
             send(part.at[kv, :, 8 + d - 4], relay_b.at[kv, i], rs_s.at[kv, 0], rs_r.at[kv, 1], at(0, d))
 
     near_slots = pl.ds(5, 7)
@@ -339,18 +344,11 @@
 
 
 def hand_on(*refs):
-    held, sem = refs[8:12], refs[12]
-    copies = [
-        (pltpu.make_async_copy(refs[i], held[i], sem.at[i]), pltpu.make_async_copy(held[i], refs[4 + i], sem.at[i]))
-        for i in range(4)
-    ]
-    for first, _ in copies:
-        first.start()
-    for first, second in copies:
-        first.wait()
-        second.start()
-    for _, second in copies:
-        second.wait()
+    copies = [pltpu.make_async_copy(refs[i], refs[4 + i], refs[8].at[i]) for i in range(4)]
+    for copy in copies:
+        copy.start()
+    for copy in copies:
+        copy.wait()
 
 
 def on_device(resp_q, resp_kv, prompt_kv, grad_out, lengths, resp_lists, owner_map):
@@ -362,13 +360,13 @@
         kernel,
         name="attention",
         out_shape=(
-            jax.ShapeDtypeStruct(resp_q.shape, BF),
-            jax.ShapeDtypeStruct(resp_q.shape, BF),
-            jax.ShapeDtypeStruct(resp_kv.shape, BF),
-            jax.ShapeDtypeStruct(prompt_kv.shape, BF),
+            pltpu.VMEM(resp_q.shape, BF),
+            pltpu.VMEM(resp_q.shape, BF),
+            pltpu.VMEM(resp_kv.shape, BF),
+            pltpu.VMEM(prompt_kv.shape, BF),
         ),
         in_specs=[anywhere] * 7,
-        out_specs=(anywhere, anywhere, anywhere, in_vmem),
+        out_specs=(in_vmem,) * 4,
         scratch_shapes=[
             pltpu.VMEM((T, rows, HW), BF),
             pltpu.VMEM((T, rows, HW), BF),
@@ -409,6 +407,7 @@
             dma((2,)),
             dma((2, 4)),
             dma((2, 5)),
+            pltpu.SemaphoreType.REGULAR,
         ],
         compiler_params=pltpu.CompilerParams(
             collective_id=0, has_side_effects=True, vmem_limit_bytes=60 * 1024 * 1024
@@ -418,11 +417,10 @@
         hand_on,
         name="hand_on",
         out_shape=tuple(jax.ShapeDtypeStruct(r.shape, r.dtype) for r in results),
-        in_specs=[anywhere] * 4,
+        in_specs=[in_vmem] * 4,
         out_specs=(anywhere,) * 4,
-        scratch_shapes=[pltpu.VMEM(r.shape, r.dtype) for r in results] + [dma((4,))],
-        compiler_params=pltpu.CompilerParams(vmem_limit_bytes=60 * 1024 * 1024),
-    )(*results)
+        scratch_shapes=[dma((4,))],
+    )(*[pltpu.with_memory_space_constraint(r, pltpu.VMEM) for r in results])
 
 
 def solution(mesh):

time: 51 us -> 48.2 us (0.945)
  Pallas kernels: 50.2 us -> 47.1 us
    pallas_call x1, Pallas kernels: 48.4 us -> 46.3 us  [on_device(): pl.pallas_call(kernel, name='attention', out_shape=(pltpu.VMEM(resp_q.sha...]
    pallas_call x1, Pallas kernels: 1.79 us -> 0.84 us  [on_device(): pl.pallas_call(hand_on, name='hand_on', out_shape=tuple((jax.ShapeDtypeSt...]
where the time goes in v5:
time: 48.2 us; the launch traced here: 47.7 us
  Pallas kernels  47.1 us (98%)
  between operations  0.64 us (1%)
    pallas_call x1, Pallas kernels, on_device(): pl.pallas_call(kernel, name='attention', out_shape=(pltpu.VMEM(resp_q.sha...  46.3 us

profile of v5, /device:TPU:1, one launch (start us, length us, event | category | flops | bytes accessed | tf_op | source)
XLA Modules:
  0.0 47.7 jit_solution(3881174114322107320)
XLA Ops:
  0.6 46.3 %attention.1 = (bf16[16,8192]{1,0:T(8,128)(2,1)S(1)}, bf16[16,8192]{1,0:T(8,128)(2,1)S(1)}, bf16[16,2048]{1,0:T(8,128)(2,1)S(1)}, bf16[32,256]{1,0:T(8,128)(2,1)S(1)}) custom-call(bf16[16,8192]{1,0:T(8,128)(2,1)} %q_in.1, bf16[16,2048]{1,0:T(8,128)(2,1)} %kv_in.1, bf16[32,256]{1,0:T(8,128)(2,1)} %pkv_in.1, bf16[16,8192]{1,0:T(8,128)(2,1)} %g_in.1, ...), custom_call_target="tpu_custom_call" | custom-call | tf_op jit(solution)/shard_map/attention/pallas_call | solution.py:359
  46.9 0.8 %hand_on.1 = (bf16[16,8192]{1,0:T(8,128)(2,1)}, bf16[16,8192]{1,0:T(8,128)(2,1)}, bf16[16,2048]{1,0:T(8,128)(2,1)}, bf16[32,256]{1,0:T(8,128)(2,1)}) custom-call(bf16[16,8192]{1,0:T(8,128)(2,1)S(1)} %get-tuple-element.8.refs_0_, bf16[16,8192]{1,0:T(8,128)(2,1)S(1)} %get-tuple-element.9.refs_1_, bf16[16,2048]{1,0:T(8,128)(2,1)S(1)} %get-tuple-element.10.refs_2_, ...), custom_call_target="tpu_custom_call" | custom-call | tf_op jit(solution)/shard_map/hand_on/pallas_call | solution.py:416

commit v6 on v5

--- a/solution.py
+++ b/solution.py
@@ -55,7 +55,8 @@
         return ((y + a - 2 * a * y) * (2 * Z) + lax.rem(z + way * d + Z, Z) * 2 + core, t)
 
     other_core = (y * (2 * Z) + z * 2 + (1 - core), t)
-    peers = [lax.rem(t + k, T) for k in range(1, T)]
+    hops = ((2, 1), (1, 1), (3, 1), (0, 1), (2, 0), (1, 0), (3, 0))
+    peers = [lax.rem(t // 2 + dx, 4) * 2 + lax.rem(t + dy, 2) for dx, dy in hops]
 
     def send(src, dst, s, r, device):
         pltpu.make_async_remote_copy(
@@ -145,7 +146,7 @@
             for b in range(BLOCKS)
         )
 
-    found = lax.fori_loop(0, 4 * Z, find, tuple(jnp.int32(0) for _ in range(SLOTS * BLOCKS)), unroll=4)
+    found = lax.fori_loop(0, 4 * Z, find, tuple(jnp.int32(0) for _ in range(SLOTS * BLOCKS)), unroll=16)
 
     def pick(cat, kv, s):
         for b in range(BLOCKS):
@@ -287,6 +288,7 @@
         hand_over(K, s, dot(dscore_t[s], stacked(qbuf, s, 0, GROUP), ((1,), (0,))))
         if s == 0:
             far(V)
+            near_y(V)
 
     results = ((obuf, att_out, HW), (dqbuf, qg_out, HW), (rgbuf, rg_out, KW))
 
@@ -311,7 +313,6 @@
                     results[a][0][4 * s : 4 * s + 4, :, head] = values.astype(BF).reshape(4, 16, HD)
 
     far(K)
-    near_y(V)
     near_y(K)
     back(0, probs_t, vcat)
     near_z(V)

time: 48.2 us -> 47.8 us (level)
  the two profiles are of different devices: /device:TPU:1 before, /device:TPU:32 now
where the time goes in v6:
time: 47.8 us; the launch traced here: 47.6 us
  Pallas kernels  47 us (98%)
  between operations  0.64 us (1%)
    pallas_call x1, Pallas kernels, on_device(): pl.pallas_call(kernel, name='attention', out_shape=(pltpu.VMEM(resp_q.sha...  46.1 us

profile of v6, /device:TPU:32, one launch (start us, length us, event | category | flops | bytes accessed | tf_op | source)
XLA Modules:
  0.0 47.6 jit_solution(8994587962011025119)
XLA Ops:
  0.6 46.1 %attention.1 = (bf16[16,8192]{1,0:T(8,128)(2,1)S(1)}, bf16[16,8192]{1,0:T(8,128)(2,1)S(1)}, bf16[16,2048]{1,0:T(8,128)(2,1)S(1)}, bf16[32,256]{1,0:T(8,128)(2,1)S(1)}) custom-call(bf16[16,8192]{1,0:T(8,128)(2,1)} %q_in.1, bf16[16,2048]{1,0:T(8,128)(2,1)} %kv_in.1, bf16[32,256]{1,0:T(8,128)(2,1)} %pkv_in.1, bf16[16,8192]{1,0:T(8,128)(2,1)} %g_in.1, ...), custom_call_target="tpu_custom_call" | custom-call | tf_op jit(solution)/shard_map/attention/pallas_call | solution.py:360
  46.8 0.8 %hand_on.1 = (bf16[16,8192]{1,0:T(8,128)(2,1)}, bf16[16,8192]{1,0:T(8,128)(2,1)}, bf16[16,2048]{1,0:T(8,128)(2,1)}, bf16[32,256]{1,0:T(8,128)(2,1)}) custom-call(bf16[16,8192]{1,0:T(8,128)(2,1)S(1)} %get-tuple-element.8.refs_0_, bf16[16,8192]{1,0:T(8,128)(2,1)S(1)} %get-tuple-element.9.refs_1_, bf16[16,2048]{1,0:T(8,128)(2,1)S(1)} %get-tuple-element.10.refs_2_, ...), custom_call_target="tpu_custom_call" | custom-call | tf_op jit(solution)/shard_map/hand_on/pallas_call | solution.py:417

commit v7 on v5

--- a/solution.py
+++ b/solution.py
@@ -38,7 +38,7 @@
     q_in, kv_in, pkv_in, g_in, lengths_in, lists_in, owners_in,
     att_out, qg_out, rg_out, pg_out,
     qbuf, gbuf, kvbuf, obuf, dqbuf, rgbuf,
-    table_k, table_v, kcat, vcat, probs_f, probs_t, dscore_t,
+    table_k, table_v, kcat, vcat, probs_t, dscore_t,
     compact_k, compact_v, part, direct, relay_a, relay_b, relayed, ypart, lengths, lists, owners,
     loc, a2a_s, a2a_r, agz_s, agz_r, agy_s, agy_r, agc_s, agc_r, back_s, back_r, cc_s, cc_r, rs_s, rs_r, heard,
 ):
@@ -200,7 +200,6 @@
             e = jnp.exp(scores - top)
             probs = e * (1.0 / jnp.sum(e, axis=0, keepdims=True))
             cols = columns(WIDE, h)
-            probs_f[s, :, cols] = probs
             probs_t[s, :, cols] = probs.astype(BF)
             return 0
 
@@ -279,8 +278,9 @@
             g = stacked(gbuf, s, h * HALF * HD, HALF)
             cols = columns(WIDE, h)
             dprob = dot(values, g, ((1,), (1,)))
-            delta = jnp.sum(probs_t[s, :, cols].astype(F32) * dprob, axis=0, keepdims=True)
-            dscore_t[s, :, cols] = (probs_f[s, :, cols] * (dprob - delta) * SCALE).astype(BF)
+            probs = probs_t[s, :, cols].astype(F32)
+            delta = jnp.sum(probs * dprob, axis=0, keepdims=True)
+            dscore_t[s, :, cols] = (probs * (dprob - delta) * SCALE).astype(BF)
             return 0
 
         lax.fori_loop(0, 2, second_pass, 0, unroll=True)
@@ -378,7 +378,6 @@
             pltpu.VMEM((2, 2, Z, BR, HD), BF),
             pltpu.VMEM((SLOTS, KEYS, HD), BF),
             pltpu.VMEM((SLOTS, KEYS, HD), BF),
-            pltpu.VMEM((SLOTS, KEYS, GROUP * LR), F32),
             pltpu.VMEM((SLOTS, KEYS, GROUP * LR), BF),
             pltpu.VMEM((SLOTS, KEYS, GROUP * LR), BF),
             pltpu.VMEM((2, SLOTS, BLOCKS, BR, HD), BF),

time: 48.2 us -> 48.2 us (level)
  no operation moved by 1% of the time
where the time goes in v7:
time: 48.2 us; the launch traced here: 47.7 us
  Pallas kernels  47.1 us (98%)
  between operations  0.64 us (1%)
    pallas_call x1, Pallas kernels, on_device(): pl.pallas_call(kernel, name='attention', out_shape=(pltpu.VMEM(resp_q.sha...  46.3 us

profile of v7, /device:TPU:1, one launch (start us, length us, event | category | flops | bytes accessed | tf_op | source)
XLA Modules:
  0.0 47.7 jit_solution(2464930177932122296)
XLA Ops:
  0.6 46.3 %attention.1 = (bf16[16,8192]{1,0:T(8,128)(2,1)S(1)}, bf16[16,8192]{1,0:T(8,128)(2,1)S(1)}, bf16[16,2048]{1,0:T(8,128)(2,1)S(1)}, bf16[32,256]{1,0:T(8,128)(2,1)S(1)}) custom-call(bf16[16,8192]{1,0:T(8,128)(2,1)} %q_in.1, bf16[16,2048]{1,0:T(8,128)(2,1)} %kv_in.1, bf16[32,256]{1,0:T(8,128)(2,1)} %pkv_in.1, bf16[16,8192]{1,0:T(8,128)(2,1)} %g_in.1, ...), custom_call_target="tpu_custom_call" | custom-call | tf_op jit(solution)/shard_map/attention/pallas_call | solution.py:359
  46.9 0.8 %hand_on.1 = (bf16[16,8192]{1,0:T(8,128)(2,1)}, bf16[16,8192]{1,0:T(8,128)(2,1)}, bf16[16,2048]{1,0:T(8,128)(2,1)}, bf16[32,256]{1,0:T(8,128)(2,1)}) custom-call(bf16[16,8192]{1,0:T(8,128)(2,1)S(1)} %get-tuple-element.8.refs_0_, bf16[16,8192]{1,0:T(8,128)(2,1)S(1)} %get-tuple-element.9.refs_1_, bf16[16,2048]{1,0:T(8,128)(2,1)S(1)} %get-tuple-element.10.refs_2_, ...), custom_call_target="tpu_custom_call" | custom-call | tf_op jit(solution)/shard_map/hand_on/pallas_call | solution.py:415
